TPU v7x, 32 devices: a whole 2x2x4 slice. The times are simulated.
32 devices in a mesh: groups: 2 (over y), level: 4 (over z), src: 2 (over x), phase: 2 (over core).
Axes of the slice: x: 2, y: 2, z: 4, core: 2. Of those that a mesh axis runs over, the one named last changes fastest.
Arguments:
- state_values: float32 [24, 8, 32, 16, 128], P(('groups', 'level'), 'src', 'phase'), parts along dimension 0, may hold values from -6 to 6
- phase_rates: float32 [64, 32], P('groups'), parts along dimension 0, may hold values from 0.05 to 2
- batch_rates: float32 [32, 32, 32], P('groups'), parts along dimension 0, may hold values from 0.02 to 1
- service_rates: float32 [4], P('groups'), parts along dimension 0, may hold values from 20 to 60
- source_rates: float32 [6, 3], P('groups'), parts along dimension 0, may hold values from 2 to 30
- tile_levels: int32 [16, 2], P('groups'), parts along dimension 0, may hold values from 0 to 3, as said below
- routes: int32 [16, 5], P('groups'), parts along dimension 0, may hold values from -1 to 7, as said below
- tile_owner: int32 [16], P('groups'), parts along dimension 0, may hold values from 0 to 11, as said below
Outputs:
- stepped_values: float32 [24, 8, 32, 16, 128], P(('groups', 'level'), 'src', 'phase'), parts along dimension 0
There are 2 independent parts, one for each index of `groups`. A program takes and returns all parts, laid end to end along the dimension named above; each array names one. Nothing has to cross between parts.
Inputs may be any that keep to these rules, and one draw needn't show every extreme that they name: `tile_levels`: row t is the tile (a, c) covering buffer-one levels a * 128 to a * 128 + 127 and buffer-two levels c * 16 to c * 16 + 15; tiles are numbered column by column (c rising, then a rising), every c from 0 to 3 has tiles a = 0, 1, ... up to its own height, and the tallest column has 3 tiles. routes[t] lists the tiles (a - 1, c), (a + 1, c), (a, c - 1), (a, c + 1) and (a + 1, c - 1) of tile t = (a, c), or -1 where no such tile exists. `tile_owner`: each tile has its own slot; slots d * 3 to d * 3 + 2 belong to index d of level. Every index holds 1 to 3 tiles, the busiest exactly 3, with consecutive tile numbers in its first slots in order. Slots that hold no tile are ignored.
All inputs are finite; a program needn't handle non-finite values.
Results may differ from a plain program's by a relative error of at most 0.0001.
Values sent between devices are 32-bit elements; how exact they have to be, the bound alone decides.
A program may use at most 128 MiB of HBM per device.

v0:
```python
import jax
import jax.numpy as jnp
from jax import lax
from jax.sharding import PartitionSpec as P

BATCH = 16
SOURCES = 3


PRECISE = lax.Precision.HIGHEST


def from_partner(x, axis, bit):
    return lax.ppermute(x, axis, [(i, i ^ 1 << bit) for i in range(lax.axis_size(axis))])


def phase_tables(phase_rates, batch_rates):
    phases = phase_rates.shape[0]
    unit_matrix = jnp.eye(phases, dtype=phase_rates.dtype)
    moving = phase_rates * (1.0 - unit_matrix)
    leaving = jnp.sum(moving, axis=1) + jnp.sum(batch_rates, axis=(0, 2))
    stacked = jnp.concatenate(
        [(moving - unit_matrix * leaving[:, None])[None], batch_rates], axis=0
    )
    return (stacked, jnp.max(leaving))


def uniform_rate(top_leaving, service_rates, source_rates):
    sources_top = jnp.sum(jnp.maximum(source_rates[:, 2] + source_rates[:, 1], source_rates[:, 0]))
    return top_leaving + service_rates[0] + service_rates[1] + sources_top


def source_terms(states, source_rates):
    powers = jnp.cumprod(jnp.full((SOURCES,), 2, jnp.int32)) // 2
    on_bits = (states[:, None] // powers[None, :] % 2).astype(source_rates.dtype)
    turn_on = source_rates[:, 0][None, :]
    turn_off = source_rates[:, 1][None, :]
    arrive = source_rates[:, 2][None, :]
    feeding = jnp.sum(on_bits * arrive, axis=1)
    incoming = on_bits * turn_on + (1.0 - on_bits) * turn_off
    outgoing = jnp.sum(on_bits * turn_off + (1.0 - on_bits) * turn_on, axis=1)
    return (feeding, incoming, outgoing)


def table_rows(lookup_table, wanted):
    flattened = lookup_table.reshape(lookup_table.shape[0], -1)
    matches = wanted[:, None] == jnp.arange(lookup_table.shape[0], dtype=jnp.int32)[None, :]
    picked = jnp.sum(jnp.where(matches[:, :, None], flattened[None, :, :], 0), axis=1)
    return picked.reshape(wanted.shape + lookup_table.shape[1:])


def edge_parts(tile_block, lower_row, upper_row, rim_depth):
    top_part = tile_block[..., tile_block.shape[-1] - rim_depth :]
    top_part = top_part.reshape(tile_block.shape[:3] + (tile_block.shape[3] * rim_depth,))
    bottom_part = jnp.concatenate([lower_row[..., 0][..., None], tile_block[..., 0]], axis=-1)
    return (top_part, bottom_part, lower_row, upper_row, lower_row[..., 0])


def pick_rows(wanted, pieces):
    row_count = pieces.shape[0]
    matches = (wanted[:, None] == jnp.arange(row_count, dtype=jnp.int32)[None, :]).astype(
        pieces.dtype
    )
    flattened = pieces.reshape(row_count, -1)
    picked = jnp.dot(matches, flattened, precision=PRECISE)
    return picked.reshape((wanted.shape[0],) + pieces.shape[1:])


def body(
    state_values,
    phase_rates,
    batch_rates,
    service_rates,
    source_rates,
    tile_levels,
    routes,
    tile_owner,
):
    slot_count, local_states, local_phases, width_two, width_one = state_values.shape
    src_rank = lax.axis_index("src")
    tables, top_leaving = phase_tables(phase_rates, batch_rates)
    uniform = uniform_rate(top_leaving, service_rates, source_rates)
    phase_start = lax.axis_index("phase") * local_phases
    tables_local = lax.dynamic_slice_in_dim(tables, phase_start, local_phases, 2)
    current = state_values
    states = src_rank * local_states + jnp.arange(local_states, dtype=jnp.int32)
    row_ids = jnp.arange(width_two, dtype=jnp.int32)
    block_states = current.shape[1]
    local_bits = block_states.bit_length() - 1
    feeding, incoming, outgoing = source_terms(states, source_rates)
    holders = lax.axis_index("level") * slot_count + jnp.arange(slot_count, dtype=jnp.int32)
    owned_here = tile_owner[None, :] == holders[:, None]
    filled = jnp.any(owned_here, axis=1)
    tile_ids = jnp.arange(tile_owner.shape[0], dtype=jnp.int32)
    my_tiles = jnp.sum(jnp.where(owned_here, tile_ids[None, :], 0), axis=1)
    my_routes = table_rows(routes, my_tiles)
    my_levels = table_rows(tile_levels, my_tiles)
    route_slots = table_rows(tile_owner, jnp.maximum(my_routes, 0).reshape(-1)).reshape(
        my_routes.shape
    )
    wanted = jnp.where((my_routes >= 0) & filled[:, None], route_slots, -1)
    first_pos = my_levels[:, 0:1] * width_one + jnp.arange(width_one, dtype=jnp.int32)[None, :] > 0
    second_pos = my_levels[:, 1:2] * width_two + row_ids[None, :] > 0
    leaving_rate = (
        service_rates[0] * first_pos[:, None, None, None, :]
        + service_rates[1] * second_pos[:, None, None, :, None]
        + (feeding + outgoing)[None, :, None, None, None]
    )
    for repeat in range(2):
        lower_row = current[..., -1, :]
        upper_row = current[..., 0, :]
        edge_sets = edge_parts(current, lower_row, upper_row, BATCH)
        pieces = (
            lax.all_gather(edge_sets[0], "level", axis=0, tiled=True),
            lax.all_gather(edge_sets[1], "level", axis=0, tiled=True),
            lax.all_gather(edge_sets[2], "level", axis=0, tiled=True),
            lax.all_gather(edge_sets[3], "level", axis=0, tiled=True),
            lax.all_gather(edge_sets[4], "level", axis=0, tiled=True),
        )
        picked = tuple((pick_rows(wanted[:, index], pieces[index]) for index in range(5)))
        full_values = lax.all_gather(current, "phase", axis=2, tiled=True)
        top_full = lax.all_gather(picked[0], "phase", axis=2, tiled=True)
        above_ext = picked[1]
        left_last = picked[2]
        right_first = picked[3]
        corner_cell = picked[4]
        above_bottom = above_ext[..., 1:]
        top_full = top_full.reshape(full_values.shape[:4] + (BATCH,))
        extended = jnp.concatenate([top_full, full_values], axis=-1)
        change = jnp.zeros(current.shape, jnp.float32)
        for offset in range(BATCH + 1):
            window = extended[..., BATCH - offset : BATCH - offset + width_one]
            change = change + jnp.einsum(
                "cspuv,pq->csquv", window, tables_local[offset], precision=PRECISE
            )
        row_ext = jnp.concatenate([current, above_bottom[..., None]], axis=-1)
        side_ext = jnp.concatenate([left_last, corner_cell[..., None]], axis=-1)
        joined = jnp.concatenate([side_ext[..., None, :], row_ext], axis=-2)
        service_one = joined[..., :width_two, 1:]
        service_two = jnp.concatenate([current, right_first[..., None, :]], axis=-2)[..., 1:, :]
        feed_two = jnp.concatenate([left_last[..., None, :], current], axis=-2)[..., :width_two, :]
        for source_bit in range(SOURCES):
            if source_bit < local_bits:
                stride = 2**source_bit
                shaped = current.reshape(
                    (slot_count, block_states // (2 * stride), 2, stride) + current.shape[2:]
                )
                partner = jnp.flip(shaped, axis=2).reshape(current.shape)
            else:
                partner = from_partner(current, "src", source_bit - local_bits)
            change = change + incoming[:, source_bit][None, :, None, None, None] * partner
        change = (
            change
            + service_rates[0] * service_one
            + service_rates[1] * service_two
            + feeding[None, :, None, None, None] * feed_two
            - leaving_rate * current
        )
        stepped = current + change / uniform
        current = jnp.where(filled[:, None, None, None, None], stepped, 0.0)
    return current


def solution(mesh):
    placed = (
        P(("groups", "level"), "src", "phase", None, None),
        P("groups", None),
        P("groups", None, None),
        P("groups"),
        P("groups", None),
        P("groups", None),
        P("groups", None),
        P("groups"),
    )
    return jax.shard_map(
        body,
        mesh=mesh,
        in_specs=placed,
        out_specs=P(("groups", "level"), "src", "phase", None, None),
        check_vma=False,
    )
```

profile of v0, /device:TPU:0, one launch (start us, length us, event | category | flops | bytes accessed | tf_op | source)
XLA Modules:
  0.0 388.1 jit_solution(14093897819066521582)
XLA Ops:
  19.0 13.4 %all-gather.1 = f32[12,4,16,1]{2,1,3,0:T(4,128)S(1)} all-gather(f32[3,4,16,1]{2,1,3,0:T(4,128)S(1)} %copy.212), channel_id=3, replica_groups=mesh['groups'=2,'level'=4,'src'=2,'phase'=2] {'level'}, dimensions={0}, use_global_device_ids=true | all-gather | bytes 3840 | tf_op jit(solution)/shard_map/all_gather | solution.py:118
  34.9 15.1 %all_gather.47 = f32[12,4,16,17]{3,2,1,0:T(8,128)S(1)} all-gather(f32[3,4,16,17]{3,2,1,0:T(8,128)S(1)} %pad_maximum_fusion.14), channel_id=1, replica_groups=mesh['groups'=2,'level'=4,'src'=2,'phase'=2] {'level'}, dimensions={0}, use_global_device_ids=true | all-gather | bytes 65280 | tf_op jit(solution)/shard_map/all_gather | solution.py:115
  54.1 15.5 %all-gather = f32[12,4,16,1,128]{4,2,3,1,0:T(8,128)S(1)} all-gather(f32[3,4,16,1,128]{4,2,3,1,0:T(8,128)} %bitcast.368), channel_id=2, replica_groups=mesh['groups'=2,'level'=4,'src'=2,'phase'=2] {'level'}, dimensions={0}, use_global_device_ids=true | all-gather | bytes 491520 | tf_op jit(solution)/shard_map/all_gather | solution.py:116
  70.9 15.4 %all-gather.2 = f32[12,4,16,1,128]{4,2,3,1,0:T(8,128)} all-gather(f32[3,4,16,1,128]{4,2,3,1,0:T(8,128)S(1)} %copy-done.12), channel_id=4, replica_groups=mesh['groups'=2,'level'=4,'src'=2,'phase'=2] {'level'}, dimensions={0}, use_global_device_ids=true | all-gather | bytes 491520 | tf_op jit(solution)/shard_map/all_gather | solution.py:117
  87.6 16.2 %all_gather.43 = f32[12,4,16,256]{3,2,1,0:T(8,128)S(1)} all-gather(f32[3,4,16,256]{3,2,1,0:T(8,128)} %reshape.284), channel_id=1, replica_groups=mesh['groups'=2,'level'=4,'src'=2,'phase'=2] {'level'}, dimensions={0}, use_global_device_ids=true | all-gather | bytes 983040 | tf_op jit(solution)/shard_map/all_gather | solution.py:114
  132.2 6.1 %fusion.49 = f32[16,3,4,16,128]{4,0,3,2,1:T(8,128)} fusion(f32[3,4,32,16,16]{4,2,3,1,0:T(8,128)S(1)} %copy.206, f32[3,4,32,16,128]{4,2,3,1,0:T(8,128)} %all-gather.9.cloned.1.call-done, f32[17,32,16]{1,2,0:T(8,128)S(1)} %fusion.128), kind=kOutput, calls=%fused_computation.93 | convolution fusion | flops 151781376 | bytes 7872512 | tf_op jit(solution)/shard_map/cspuv,pq->csquv/dot_general | solution.py:133
  138.2 4.1 %fusion.52 = f32[16,3,4,16,128]{4,0,3,2,1:T(8,128)} fusion(f32[3,4,32,16,16]{4,2,3,1,0:T(8,128)S(1)} %copy.206, f32[3,4,32,16,128]{4,2,3,1,0:T(8,128)S(1)} %copy-done, f32[17,32,16]{1,2,0:T(8,128)S(1)} %fusion.128), kind=kOutput, calls=%fused_computation.95 | convolution fusion | flops 151781376 | bytes 7872512 | tf_op jit(solution)/shard_map/cspuv,pq->csquv/dot_general | solution.py:133
  146.3 4.3 %fusion.58 = f32[16,3,4,16,128]{4,0,3,2,1:T(8,128)} fusion(f32[3,4,32,16,16]{4,2,3,1,0:T(8,128)S(1)} %copy.206, f32[3,4,32,16,128]{4,2,3,1,0:T(8,128)S(1)} %copy-done, f32[17,32,16]{1,2,0:T(8,128)S(1)} %fusion.128), kind=kOutput, calls=%fused_computation.99 | convolution fusion | flops 151781376 | bytes 7872512 | tf_op jit(solution)/shard_map/cspuv,pq->csquv/dot_general | solution.py:133
  154.6 4.1 %fusion.64 = f32[16,3,4,16,128]{4,0,3,2,1:T(8,128)} fusion(f32[3,4,32,16,16]{4,2,3,1,0:T(8,128)S(1)} %copy.206, f32[3,4,32,16,128]{4,2,3,1,0:T(8,128)S(1)} %copy-done, f32[17,32,16]{1,2,0:T(8,128)S(1)} %fusion.128), kind=kOutput, calls=%fused_computation.103 | convolution fusion | flops 151781376 | bytes 7872512 | tf_op jit(solution)/shard_map/cspuv,pq->csquv/dot_general | solution.py:133
  158.7 4.0 %fusion.67 = f32[16,3,4,16,128]{4,0,3,2,1:T(8,128)} fusion(f32[3,4,32,16,16]{4,2,3,1,0:T(8,128)S(1)} %copy.206, f32[3,4,32,16,128]{4,2,3,1,0:T(8,128)S(1)} %copy-done, f32[17,32,16]{1,2,0:T(8,128)S(1)} %fusion.128), kind=kOutput, calls=%fused_computation.105 | convolution fusion | flops 151781376 | bytes 7872512 | tf_op jit(solution)/shard_map/cspuv,pq->csquv/dot_general | solution.py:133
  162.7 4.4 %fusion.70 = f32[16,3,4,16,128]{4,0,3,2,1:T(8,128)} fusion(f32[3,4,32,16,16]{4,2,3,1,0:T(8,128)S(1)} %copy.206, f32[3,4,32,16,128]{4,2,3,1,0:T(8,128)S(1)} %copy-done, f32[17,32,16]{1,2,0:T(8,128)S(1)} %fusion.128), kind=kOutput, calls=%fused_computation.107 | convolution fusion | flops 151781376 | bytes 7872512 | tf_op jit(solution)/shard_map/cspuv,pq->csquv/dot_general | solution.py:133
  167.1 4.0 %fusion.73 = f32[16,3,4,16,128]{4,0,3,2,1:T(8,128)} fusion(f32[3,4,32,16,16]{4,2,3,1,0:T(8,128)S(1)} %copy.206, f32[3,4,32,16,128]{4,2,3,1,0:T(8,128)S(1)} %copy-done, f32[17,32,16]{1,2,0:T(8,128)S(1)} %fusion.128), kind=kOutput, calls=%fused_computation.109 | convolution fusion | flops 151781376 | bytes 7872512 | tf_op jit(solution)/shard_map/cspuv,pq->csquv/dot_general | solution.py:133
  179.2 4.0 %fusion.82 = f32[16,3,4,16,128]{4,0,3,2,1:T(8,128)} fusion(f32[3,4,32,16,16]{4,2,3,1,0:T(8,128)S(1)} %copy.206, f32[3,4,32,16,128]{4,2,3,1,0:T(8,128)S(1)} %copy-done, f32[17,32,16]{1,2,0:T(8,128)S(1)} %fusion.128), kind=kOutput, calls=%fused_computation.115 | convolution fusion | flops 151781376 | bytes 7872512 | tf_op jit(solution)/shard_map/cspuv,pq->csquv/dot_general | solution.py:133
  183.2 4.2 %fusion.85 = f32[16,3,4,16,128]{4,0,3,2,1:T(8,128)} fusion(f32[3,4,32,16,16]{4,2,3,1,0:T(8,128)S(1)} %copy.206, f32[3,4,32,16,128]{4,2,3,1,0:T(8,128)S(1)} %copy-done, f32[17,32,16]{1,2,0:T(8,128)S(1)} %fusion.128), kind=kOutput, calls=%fused_computation.117 | convolution fusion | flops 151781376 | bytes 7872512 | tf_op jit(solution)/shard_map/cspuv,pq->csquv/dot_general | solution.py:133
  191.4 4.0 %fusion.46 = f32[16,3,4,16,128]{4,0,3,2,1:T(8,128)} fusion(f32[3,4,32,16,16]{4,2,3,1,0:T(8,128)S(1)} %copy.206, f32[3,4,32,16,128]{4,2,3,1,0:T(8,128)S(1)} %copy-done, f32[17,32,16]{1,2,0:T(8,128)S(1)} %fusion.128), kind=kOutput, calls=%fused_computation.91 | convolution fusion | flops 151781376 | bytes 7872512 | tf_op jit(solution)/shard_map/cspuv,pq->csquv/dot_general | solution.py:133
  198.2 15.3 %fusion.109 = f32[3,4,16,16,128]{4,2,3,1,0:T(8,128)} fusion(f32[3,4,16,16,128]{4,2,3,1,0:T(8,128)S(1)} %copy-done.3, f32[3,4,16,1,128]{4,2,3,1,0:T(8,128)S(1)} %bitcast.372, f32[3,4,16,1,128]{4,2,3,1,0:T(8,128)} %bitcast.377, f32[3,4,16,1,129]{4,2,3,1,0:T(8,128)} %maximum_bitcast_fusion, f32[3,4,16,16,1]{4,2,3,1,0:T(8,128)} %copy.220, ...), kind=kOutput, calls=%fused_computation.146 | convolution fusion | flops 166330368 | bytes 39738636 | tf_op jit(solution)/shard_map/cspuv,pq->csquv/dot_general | solution.py:133
  219.7 13.1 %all-gather.4 = f32[12,4,16,1]{2,1,3,0:T(4,128)S(1)} all-gather(f32[3,4,16,1]{2,1,3,0:T(4,128)S(1)} %copy.232), channel_id=6, replica_groups=mesh['groups'=2,'level'=4,'src'=2,'phase'=2] {'level'}, dimensions={0}, use_global_device_ids=true | all-gather | bytes 3840 | tf_op jit(solution)/shard_map/all_gather | solution.py:118
  234.2 15.1 %all_gather.54 = f32[12,4,16,17]{3,2,1,0:T(8,128)S(1)} all-gather(f32[3,4,16,17]{3,2,1,0:T(8,128)S(1)} %pad_maximum_fusion.15), channel_id=1, replica_groups=mesh['groups'=2,'level'=4,'src'=2,'phase'=2] {'level'}, dimensions={0}, use_global_device_ids=true | all-gather | bytes 65280 | tf_op jit(solution)/shard_map/all_gather | solution.py:115
  250.0 15.3 %all-gather.5 = f32[12,4,16,1,128]{4,2,3,1,0:T(8,128)S(1)} all-gather(f32[3,4,16,1,128]{4,2,3,1,0:T(8,128)S(1)} %get-tuple-element.15), channel_id=7, replica_groups=mesh['groups'=2,'level'=4,'src'=2,'phase'=2] {'level'}, dimensions={0}, use_global_device_ids=true | all-gather | bytes 491520 | tf_op jit(solution)/shard_map/all_gather | solution.py:117
  266.4 14.3 %all-gather.3 = f32[12,4,16,1,128]{4,2,3,1,0:T(8,128)S(1)} all-gather(f32[3,4,16,1,128]{4,2,3,1,0:T(8,128)S(1)} %get-tuple-element.16), channel_id=5, replica_groups=mesh['groups'=2,'level'=4,'src'=2,'phase'=2] {'level'}, dimensions={0}, use_global_device_ids=true | all-gather | bytes 491520 | tf_op jit(solution)/shard_map/all_gather | solution.py:116
  290.9 15.8 %all_gather.50 = f32[12,4,16,256]{3,2,1,0:T(8,128)S(1)} all-gather(f32[3,4,16,256]{3,2,1,0:T(8,128)S(1)} %reshape.298), channel_id=1, replica_groups=mesh['groups'=2,'level'=4,'src'=2,'phase'=2] {'level'}, dimensions={0}, use_global_device_ids=true | all-gather | bytes 983040 | tf_op jit(solution)/shard_map/all_gather | solution.py:114
  315.6 4.9 %fusion.4 = f32[16,3,4,16,128]{4,0,3,2,1:T(8,128)S(1)} fusion(f32[3,4,32,16,16]{4,2,3,1,0:T(8,128)S(1)} %copy.231, f32[3,4,32,16,128]{4,2,3,1,0:T(8,128)} %all-gather.11.cloned.1.call-done, f32[17,32,16]{1,2,0:T(8,128)S(1)} %fusion.128), kind=kOutput, calls=%fused_computation.63 | convolution fusion | flops 151781376 | bytes 7872512 | tf_op jit(solution)/shard_map/cspuv,pq->csquv/dot_general | solution.py:133
  352.8 4.2 %fusion.40 = f32[16,3,4,16,128]{4,0,3,2,1:T(8,128)} fusion(f32[3,4,32,16,16]{4,2,3,1,0:T(8,128)S(1)} %copy.231, f32[3,4,32,16,128]{4,2,3,1,0:T(8,128)S(1)} %copy-done.1, f32[17,32,16]{1,2,0:T(8,128)S(1)} %fusion.128), kind=kOutput, calls=%fused_computation.87 | convolution fusion | flops 151781376 | bytes 7872512 | tf_op jit(solution)/shard_map/cspuv,pq->csquv/dot_general | solution.py:133
  370.8 8.7 %fusion.99 = f32[3,4,16,16,128]{4,2,3,1,0:T(8,128)S(1)} fusion(f32[3,4,16,16,128]{4,2,3,1,0:T(8,128)} %fusion.109, f32[3,4,16,1,128]{4,2,3,1,0:T(8,128)S(1)} %bitcast.374, f32[3,4,16,1,128]{4,2,3,1,0:T(8,128)} %bitcast.378, f32[3,4,16,1,129]{4,2,3,1,0:T(8,128)} %maximum_bitcast_fusion.1, f32[3,4,16,16,1]{4,2,3,1,0:T(8,128)S(1)} %copy-done.6, ...), kind=kLoop, calls=%fused_computation.132 | loop fusion | flops 14548992 | bytes 35009360 | tf_op jit(solution)/shard_map/jit(_where)/select_n | solution.py:160
  (194 shorter events, 145.6 us)
Async XLA Ops:
  6.5 6.6 %copy-start.2 = (f32[3,4,16,16,128]{4,3,2,1,0:T(8,128)S(1)}, f32[3,4,16,16,128]{4,3,2,1,0:T(8,128)}, u32[]{:S(2)}) copy-start(f32[3,4,16,16,128]{4,3,2,1,0:T(8,128)} %param.8) | copy-start | bytes 4718596
  6.5 125.6 %all-gather.9.cloned.1.call-start = ((), (), s32[]{:S(2)}) async-start(), calls=%async_computation | async-start | bytes 4718592 | tf_op jit(solution)/shard_map/all_gather | solution.py:121
  9.7 7.3 %copy-start.23 = (s32[8,5]{1,0:T(8,128)S(1)}, s32[8,5]{1,0:T(8,128)}, u32[]{:S(2)}) copy-start(s32[8,5]{1,0:T(8,128)} %param.14) | copy-start | bytes 484
  9.7 8.5 %copy-start.15 = (f32[32,32]{1,0:T(8,128)S(1)}, f32[32,32]{1,0:T(8,128)}, u32[]{:S(2)}) copy-start(f32[32,32]{1,0:T(8,128)} %param.9) | copy-start | bytes 12292
  9.7 305.9 %all-gather.11.cloned.1.call-start = ((), (), s32[]{:S(2)}) async-start(), calls=%async_computation.1 | async-start | bytes 4718592 | tf_op jit(solution)/shard_map/all_gather | solution.py:121
  9.8 188.4 %collective-permute-start = (f32[3,4,16,16,128]{4,2,3,1,0:T(8,128)}, f32[3,4,16,16,128]{4,2,3,1,0:T(8,128)}, u32[]{:S(2)}, u32[]{:S(2)}) collective-permute-start(f32[3,4,16,16,128]{4,2,3,1,0:T(8,128)} %copy.227), channel_id=1, source_target_pairs={{0,2},{2,0},{1,3},{3,1},{4,6},{6,4},{5,7},{7,5},{8,10},{10,8},{9,1... | collective-permute-start | bytes 4718600 | tf_op jit(solution)/shard_map/ppermute | solution.py:14
  13.3 21.5 %copy-start.7 = (f32[3,4,16,1,128]{4,3,2,1,0:T(1,128)}, f32[3,4,16,1,128]{4,3,2,1,0:T(1,128)S(1)}, u32[]{:S(2)}) copy-start(f32[3,4,16,1,128]{4,3,2,1,0:T(1,128)S(1)} %slice.324) | copy-start | bytes 294916
  15.4 19.4 %copy-start.25 = (pred[3,8]{1,0:T(4,128)(4,1)}, pred[3,8]{1,0:T(4,128)(4,1)S(1)}, u32[]{:S(2)}) copy-start(pred[3,8]{1,0:T(4,128)(4,1)S(1)} %iota_compare_fusion.9) | copy-start | bytes 76
  18.2 16.6 %copy-start.29 = (s32[3]{0:T(128)}, s32[3]{0:T(128)S(1)}, u32[]{:S(2)}) copy-start(s32[3]{0:T(128)S(1)} %get-tuple-element.20) | copy-start | bytes 40
  18.2 51.7 %copy-start.20 = (s32[3]{0:T(128)}, s32[3]{0:T(128)S(1)}, u32[]{:S(2)}) copy-start(s32[3]{0:T(128)S(1)} %get-tuple-element.21) | copy-start | bytes 40
  18.2 87.2 %copy-start.16 = (s32[3]{0:T(128)}, s32[3]{0:T(128)S(1)}, u32[]{:S(2)}) copy-start(s32[3]{0:T(128)S(1)} %get-tuple-element.17) | copy-start | bytes 40
  18.2 88.8 %copy-start.18 = (s32[3]{0:T(128)}, s32[3]{0:T(128)S(1)}, u32[]{:S(2)}) copy-start(s32[3]{0:T(128)S(1)} %get-tuple-element.19) | copy-start | bytes 40
  52.9 18.0 %copy-start.12 = (f32[3,4,16,1,128]{4,2,3,1,0:T(8,128)S(1)}, f32[3,4,16,1,128]{4,2,3,1,0:T(8,128)}, u32[]{:S(2)}) copy-start(f32[3,4,16,1,128]{4,2,3,1,0:T(8,128)} %slice.415) | copy-start | bytes 294916
  116.4 6.4 %copy-start.13 = (f32[32,32]{0,1:T(8,128)S(1)}, f32[32,32]{0,1:T(8,128)}, u32[]{:S(2)}) copy-start(f32[32,32]{0,1:T(8,128)} %copy.198) | copy-start | bytes 12292
  116.4 6.4 %copy-start.24 = (f32[32]{0:T(128)S(1)}, f32[32]{0:T(128)}, u32[]{:S(2)}) copy-start(f32[32]{0:T(128)} %reduce_sum.82) | copy-start | bytes 388
  116.5 10.5 %copy-start.26 = (pred[3,8]{1,0:T(4,128)(4,1)S(1)}, pred[3,8]{1,0:T(4,128)(4,1)}, u32[]{:S(2)}) copy-start(pred[3,8]{1,0:T(4,128)(4,1)} %copy-done.25) | copy-start | bytes 76
  116.5 10.5 %copy-start.28 = (s32[8,2]{0,1:T(2,128)S(1)}, s32[8,2]{0,1:T(2,128)}, u32[]{:S(2)}) copy-start(s32[8,2]{0,1:T(2,128)} %param.13) | copy-start | bytes 196
  116.5 10.9 %copy-start.9 = (f32[16,32,32]{1,2,0:T(8,128)S(1)}, f32[16,32,32]{1,2,0:T(8,128)}, u32[]{:S(2)}) copy-start(f32[16,32,32]{1,2,0:T(8,128)} %copy.199) | copy-start | bytes 196612
  213.5 19.5 %copy-start.30 = (s32[3]{0:T(128)S(1)}, s32[3]{0:T(128)}, u32[]{:S(2)}) copy-start(s32[3]{0:T(128)} %copy-done.29) | copy-start | bytes 40
  215.4 49.9 %copy-start.22 = (s32[3]{0:T(128)S(1)}, s32[3]{0:T(128)}, u32[]{:S(2)}) copy-start(s32[3]{0:T(128)} %get-tuple-element.18) | copy-start | bytes 40
  215.4 154.7 %collective-permute-start.1 = (f32[3,4,16,16,128]{4,2,3,1,0:T(8,128)}, f32[3,4,16,16,128]{4,2,3,1,0:T(8,128)}, u32[]{:S(2)}, u32[]{:S(2)}) collective-permute-start(f32[3,4,16,16,128]{4,2,3,1,0:T(8,128)} %fusion.109), channel_id=1, source_target_pairs={{0,2},{2,0},{1,3},{3,1},{4,6},{6,4},{5,7},{7,5},{8,10},{10,8},{9,1... | collective-permute-start | bytes 4718600 | tf_op jit(solution)/shard_map/ppermute | solution.py:14
  234.1 47.1 %copy-start.21 = (s32[3]{0:T(128)S(1)}, s32[3]{0:T(128)}, u32[]{:S(2)}) copy-start(s32[3]{0:T(128)} %copy-done.20) | copy-start | bytes 40
  249.2 32.3 %copy-start.19 = (s32[3]{0:T(128)S(1)}, s32[3]{0:T(128)}, u32[]{:S(2)}) copy-start(s32[3]{0:T(128)} %copy-done.18) | copy-start | bytes 40
  289.7 17.0 %copy-start.17 = (s32[3]{0:T(128)S(1)}, s32[3]{0:T(128)}, u32[]{:S(2)}) copy-start(s32[3]{0:T(128)} %copy-done.16) | copy-start | bytes 40
  (13 other events, 50.3 us)
Sparse Core Ops, SparseCore 0:
  9.9 14.8 all-gather.8
  213.6 12.5 all-gather.10
where the time goes:
time: 396 us; the launch traced here: 388 us
  blocking collectives  154 us (39%)
  matrix products  142 us (36%)
  local copies, waits for them, and re-layouts  52.6 us (13%)
  other arithmetic  19 us (5%)
  between operations  16.9 us (4%)
    dot_general x34, matrix products, body(): jnp.einsum('cspuv,pq->csquv', window, tables_local[offset], precision=PRE...  136 us
    all_gather x2, blocking collectives, body(): lax.all_gather(edge_sets[0], 'level', axis=0, tiled=True)  32.1 us
    all_gather x2, blocking collectives, body(): lax.all_gather(edge_sets[3], 'level', axis=0, tiled=True)  30.7 us
    all_gather x2, blocking collectives, body(): lax.all_gather(edge_sets[1], 'level', axis=0, tiled=True)  30.2 us
    all_gather x2, blocking collectives, body(): lax.all_gather(edge_sets[2], 'level', axis=0, tiled=True)  29.8 us
    all_gather x2, blocking collectives, body(): lax.all_gather(edge_sets[4], 'level', axis=0, tiled=True)  26.5 us
    select_n x1, other arithmetic, body(): current = jnp.where(filled[:, None, None, None, None], stepped, 0.0)  8.72 us
    unnamed x77, local copies, waits for them, and re-layouts  8.13 us
  transfers between devices with their start and end apart: 4, of which 0 were waited for; matrix products, arithmetic and copies ran while one was open for 47% of the time, Pallas kernels for 0%

commit v1 on v0

v1 whole, which is shorter than its diff:
```python
import functools

import jax
import jax.numpy as jnp
import numpy as np
from jax import lax
from jax.experimental import pallas as pl
from jax.experimental.pallas import tpu as pltpu
from jax.sharding import PartitionSpec as P

SOURCES = 3
MESH = pl.DeviceIdType.MESH


def split(values):
    high = values.astype(jnp.bfloat16)
    low = (values - high.astype(jnp.float32)).astype(jnp.bfloat16)
    return high, low


def kernel(
    sizes,
    coef,
    leave,
    spots,
    x_ref,
    band_ref,
    out_ref,
    far,
    near,
    mixed,
    high,
    low,
    conv,
    band_cat,
    rows_one,
    rows_two,
    rims_one,
    rims_two,
    bots_one,
    bots_two,
    picks,
    far_send,
    far_recv,
    near_send,
    near_recv,
    pick_send,
    pick_recv,
    edge_send,
    edge_recv,
):
    n_level, n_phase, masks, local_bits, cross, fields = sizes
    C, S, Q, U, V = x_ref.shape
    SU = S * U
    CSU = C * SU
    B = rims_one.shape[-2]
    G = rims_one.shape[-1] // SU
    groups = Q // G
    lanes = G * SU
    level, src, phase = (lax.axis_index(n) for n in ("level", "src", "phase"))
    others = [{"level": lax.rem(level + r, n_level)} for r in range(1, n_level)]
    cores = [{"phase": lax.rem(phase + r, n_phase)} for r in range(1, n_phase)]
    fars = [{"src": jnp.bitwise_xor(src, m)} for m in masks]

    barrier = pltpu.get_barrier_semaphore()
    for device in others + cores + fars:
        pl.semaphore_signal(barrier, inc=1, device_id=device, device_id_type=MESH)
    pl.semaphore_wait(barrier, len(others) + len(cores) + len(fars))

    def send(source, target, sems, index, device):
        copy = pltpu.make_async_remote_copy(
            src_ref=source,
            dst_ref=target,
            send_sem=sems[0].at[index],
            recv_sem=sems[1].at[index],
            device_id=device,
            device_id_type=MESH,
        )
        copy.start()
        return copy

    near_sems = (near_send, near_recv)

    def send_near(source, step):
        return [
            send(source, near.at[step, r], near_sems, step * (n_phase - 1) + r, device)
            for r, device in enumerate(cores)
        ]

    near_copies = send_near(x_ref, 0)
    far_copies = [
        send(x_ref, far.at[m], (far_send, far_recv), m, device) for m, device in enumerate(fars)
    ]

    band_high, band_low = split(band_ref[...])
    M = band_ref.shape[0]
    band_cat[0:M, :] = band_high
    band_cat[M:, :] = band_low

    def put(i, g, first, block):
        turned = block.reshape(CSU, V).T
        top, rest = split(turned)
        at = first + i * G + g
        high[at, B:, :] = top
        low[at, B:, :] = rest
        return turned

    own = pl.ds(level * C, C)
    for step in range(2):
        field = x_ref if step == 0 else mixed
        if step == 1:
            near_copies = send_near(mixed, 1)
        rows, rims, bots = ((rows_one, rims_one, bots_one), (rows_two, rims_two, bots_two))[step]

        def fill_rows(c, carry):
            for s in range(S):
                rows[level * C + c, 0, s] = field[c, s, :, U - 1, :]
                rows[level * C + c, 1, s] = field[c, s, :, 0, :]
                if step == 1:
                    total = jnp.zeros((Q, V), jnp.float32)
                    for k in range(len(cross)):
                        total = total + coef[s * fields + 2 + SOURCES + len(cross) + k + 2] * (
                            far[k, c, s, :, U - 1, :]
                        )
                    rows[level * C + c, 2, s] = total
            return carry

        lax.fori_loop(0, C, fill_rows, 0)

        def turn_own(i, carry):
            turned = [put(i, g, 0, field[:, :, i * G + g]) for g in range(G)]
            for c in range(C):
                part = slice(c * SU, (c + 1) * SU)
                rims[level * C + c, i] = jnp.concatenate(
                    [t[V - B :, part] for t in turned], axis=1
                )
                bots[level * C + c, pl.ds(i, 1), :] = jnp.concatenate(
                    [t[0:1, part] for t in turned], axis=1
                )
            return carry

        lax.fori_loop(0, groups, turn_own, 0)

        edge_copies = []
        for r, device in enumerate(others):
            for a, ref in enumerate(
                (rims.at[own], bots.at[own], rows.at[own])
            ):
                index = (step * (n_level - 1) + r) * 3 + a
                edge_copies.append(send(ref, ref, (edge_send, edge_recv), index, device))

        for r, copy in enumerate(near_copies):
            copy.wait_recv()

            def turn_near(i, carry):
                for g in range(G):
                    put(i, g, (r + 1) * Q, near[step, r, :, :, i * G + g])
                return carry

            lax.fori_loop(0, groups, turn_near, 0)

        for copy in edge_copies:
            copy.wait_recv()

        def spread(i, first, values):
            for g in range(G):
                whole = jnp.concatenate([v[:, g * SU : (g + 1) * SU] for v in values], axis=1)
                top, rest = split(whole)
                high[first + i * G + g, 0:B, :] = top
                low[first + i * G + g, 0:B, :] = rest

        def pick(i, carry):
            values = []
            for c in range(C):
                want = spots[c * 8]
                found = rims[jnp.maximum(want, 0), i]
                value = jnp.where(want >= 0, found, 0.0)
                picks[step, 0, c, i] = value
                values.append(value)
            spread(i, 0, values)
            return carry

        lax.fori_loop(0, groups, pick, 0)
        pick_copies = [
            send(
                picks.at[step, 0],
                picks.at[step, r + 1],
                (pick_send, pick_recv),
                step * (n_phase - 1) + r,
                device,
            )
            for r, device in enumerate(cores)
        ]
        for r, copy in enumerate(pick_copies):
            copy.wait_recv()

            def take(i, carry):
                spread(i, (r + 1) * Q, [picks[step, r + 1, c, i] for c in range(C)])
                return carry

            lax.fori_loop(0, groups, take, 0)

        K = band_ref.shape[1]

        def multiply(v, carry):
            window = pl.ds(pl.multiple_of(v * B, B), 2 * B)
            top = high[:, window, :].reshape(K, CSU)
            rest = low[:, window, :].reshape(K, CSU)
            both = jnp.dot(band_cat[...], top, preferred_element_type=jnp.float32)
            third = jnp.dot(band_cat[0:M, :], rest, preferred_element_type=jnp.float32)
            total = both[0:M] + (both[M:] + third)
            conv[:, pl.ds(pl.multiple_of(v * B, B), B), :] = total.reshape(Q, B, CSU)
            return carry

        lax.fori_loop(0, V // B, multiply, 0)

        def rim_above(i, carry):
            lane = lax.broadcasted_iota(jnp.int32, (8, lanes), 1)
            values = []
            for c in range(C):
                up, corner = spots[c * 8 + 1], spots[c * 8 + 4]
                up_row = jnp.where(up >= 0, bots[jnp.maximum(up, 0), pl.ds(i, 1), :], 0.0)
                corner_row = jnp.where(
                    corner >= 0, bots[jnp.maximum(corner, 0), pl.ds(i, 1), :], 0.0
                )
                up_row = pltpu.roll(jnp.broadcast_to(up_row, (8, lanes)), 1, 1)
                corner_row = pltpu.roll(
                    jnp.broadcast_to(corner_row, (8, lanes)), lanes - (U - 1), 1
                )
                values.append(jnp.where(lane % U == 0, corner_row, up_row))
            for g in range(G):
                whole = jnp.concatenate([v[:, g * SU : (g + 1) * SU] for v in values], axis=1)
                q = i * G + g
                conv[q, V - 1 : V, :] = conv[q, V - 1 : V, :] + coef[0] * whole[0:1]
            return carry

        lax.fori_loop(0, groups, rim_above, 0)

        if step == 0:
            for copy in far_copies:
                copy.wait_recv()

        def combine(q, carry):
            back = conv[q].T
            line = lax.broadcasted_iota(jnp.int32, (U, V), 0)
            lane = lax.broadcasted_iota(jnp.int32, (U, V), 1)
            at = pl.ds(q, 1)

            def side(spot, kind, s):
                found = rows[jnp.maximum(spot, 0), kind, s, at, :]
                return jnp.broadcast_to(jnp.where(spot >= 0, found, 0.0), (U, V))

            for c in range(C):
                base = c * 8
                left, right = spots[base + 2], spots[base + 3]
                gone = (
                    leave[q]
                    + jnp.where(spots[base + 5] * V + lane > 0, coef[0], 0.0)
                    + jnp.where(spots[base + 6] * U + line > 0, coef[1], 0.0)
                )
                blocks = [field[c, s, q] for s in range(S)]
                for s in range(S):
                    here = blocks[s]
                    o = s * fields + 2
                    block = c * S + s
                    value = here + back[block * U : (block + 1) * U]
                    before = jnp.where(line == 0, side(left, 0, s), pltpu.roll(here, 1, 0))
                    after = jnp.where(line == U - 1, side(right, 1, s), pltpu.roll(here, U - 1, 0))
                    moved = jnp.where(lane == V - 1, 0.0, pltpu.roll(before, V - 1, 1))
                    value = value + coef[0] * moved + coef[1] * after + coef[o] * before
                    value = value - (gone + coef[o + 1]) * here
                    for k in range(local_bits):
                        value = value + coef[o + 2 + k] * blocks[s ^ (1 << k)]
                    o = o + 2 + SOURCES
                    n = len(cross)
                    if step == 0:
                        for k in range(n):
                            value = value + coef[o + k] * far[k, c, s, q]
                        mixed[c, s, q] = value
                    else:
                        shifted = jnp.zeros((U, V), jnp.float32)
                        for k in range(n):
                            shifted = shifted + coef[o + n + k] * far[k, c, s, q]
                            value = value + coef[o + 2 * n + k] * far[k, c, s, q]
                        if n:
                            shifted = jnp.where(
                                line == 0, side(left, 2, s), pltpu.roll(shifted, 1, 0)
                            )
                            value = value + shifted + coef[o + 3 * n] * x_ref[c, s, q]
                        for k in range(n, len(masks)):
                            value = value + coef[o + 3 * n + 1 + k - n] * far[k, c, s, q]
                        out_ref[c, s, q] = jnp.where(spots[base + 7] > 0, value, 0.0)
            return carry

        lax.fori_loop(0, Q, combine, 0)
        for copy in near_copies + edge_copies + pick_copies:
            copy.wait_send()
    for copy in far_copies:
        copy.wait_send()


def body(
    n_level,
    n_src,
    n_phase,
    state_values,
    phase_rates,
    batch_rates,
    service_rates,
    source_rates,
    tile_levels,
    routes,
    tile_owner,
):
    C, S, Q, U, V = state_values.shape
    phases = phase_rates.shape[0]
    batch = batch_rates.shape[0]
    local_bits = S.bit_length() - 1
    cross = list(range(local_bits, SOURCES))
    masks = [1 << (k - local_bits) for k in cross]
    pairs = [(a, b) for i, a in enumerate(cross) for b in cross[i + 1 :]]
    masks = masks + [(1 << (a - local_bits)) | (1 << (b - local_bits)) for a, b in pairs]

    moving = phase_rates * (1.0 - jnp.eye(phases, dtype=jnp.float32))
    leaving = jnp.sum(moving, axis=1) + jnp.sum(batch_rates, axis=(0, 2))
    turn_on, turn_off, arrive = source_rates[:, 0], source_rates[:, 1], source_rates[:, 2]
    uniform = (
        jnp.max(leaving)
        + service_rates[0]
        + service_rates[1]
        + jnp.sum(jnp.maximum(arrive + turn_off, turn_on))
    )
    part = lax.axis_index("phase") * Q
    tables = jnp.concatenate([moving[None], batch_rates], axis=0) / uniform
    tables = jnp.roll(lax.dynamic_slice_in_dim(tables, part, Q, 2), -part, axis=1)
    steps = np.arange(batch)[:, None] - np.arange(2 * batch)[None, :] + batch
    hot = (np.arange(batch + 1)[:, None, None] == steps[None]).astype(np.float32)
    band = jnp.einsum("bpq,bvw->qvpw", tables, hot, precision=lax.Precision.HIGHEST)
    band = band.reshape(Q * batch, phases * 2 * batch)
    leave = lax.dynamic_slice_in_dim(leaving, part, Q, 0) / uniform

    states = lax.axis_index("src") * S + jnp.arange(S, dtype=jnp.int32)
    bits = ((states[:, None] >> np.arange(SOURCES, dtype=np.int32)[None, :]) & 1) == 1
    feed = jnp.sum(jnp.where(bits, arrive[None], 0.0), axis=1) / uniform
    inflow = jnp.where(bits, turn_on[None], turn_off[None]) / uniform
    outs = jnp.where(bits, turn_off[None], turn_on[None]) / uniform
    out = jnp.sum(outs, axis=1)
    more_feed = jnp.where(bits, -arrive[None], arrive[None]) / uniform
    more_out = inflow - outs
    columns = [feed, feed + out] + [inflow[:, k] for k in range(SOURCES)]
    columns += [2.0 * inflow[:, k] for k in cross]
    columns += [inflow[:, k] * more_feed[:, k] for k in cross]
    columns += [-inflow[:, k] * (more_feed[:, k] + more_out[:, k]) for k in cross]
    columns += [sum((inflow[:, k] * outs[:, k] for k in cross), jnp.zeros((S,), jnp.float32))]
    columns += [2.0 * inflow[:, a] * inflow[:, b] for a, b in pairs]
    fields = len(columns)
    coef = jnp.concatenate([service_rates / uniform, jnp.stack(columns, axis=1).reshape(-1)])

    holders = lax.axis_index("level") * C + jnp.arange(C, dtype=jnp.int32)
    owned = (tile_owner[None, :] == holders[:, None]).astype(jnp.int32)
    filled = jnp.sum(owned, axis=1)
    slots = jnp.sum(
        jnp.where(
            routes[:, :, None] == jnp.arange(tile_owner.shape[0], dtype=jnp.int32),
            tile_owner[None, None, :] + 1,
            0,
        ),
        axis=2,
    )
    known = jnp.concatenate([slots, tile_levels], axis=1)
    mine = jnp.sum(owned[:, :, None] * known[None], axis=1)
    spots = jnp.concatenate([mine[:, :5] - 1, mine[:, 5:], filled[:, None]], axis=1).reshape(-1)

    group = min(Q, max(1, 128 // (S * U)))
    slot_count = n_level * C
    f32, bf16 = jnp.float32, jnp.bfloat16
    sems = pltpu.SemaphoreType.DMA
    sizes = (n_level, n_phase, masks, local_bits, cross, fields)
    vmem = pl.BlockSpec(memory_space=pltpu.VMEM)
    smem = pl.BlockSpec(memory_space=pltpu.SMEM)
    near_count = max(1, n_phase - 1)
    edge_count = max(1, 6 * (n_level - 1))
    return pl.pallas_call(
        functools.partial(kernel, sizes),
        out_shape=jax.ShapeDtypeStruct(state_values.shape, f32),
        in_specs=[smem, smem, smem, vmem, vmem],
        out_specs=vmem,
        scratch_shapes=[
            pltpu.VMEM((max(1, len(masks)),) + state_values.shape, f32),
            pltpu.VMEM((2, near_count) + state_values.shape, f32),
            pltpu.VMEM(state_values.shape, f32),
            pltpu.VMEM((phases, batch + V, C * S * U), bf16),
            pltpu.VMEM((phases, batch + V, C * S * U), bf16),
            pltpu.VMEM((Q, V, C * S * U), f32),
            pltpu.VMEM((2 * Q * batch, phases * 2 * batch), bf16),
            pltpu.VMEM((slot_count, 2, S, Q, V), f32),
            pltpu.VMEM((slot_count, 3, S, Q, V), f32),
            pltpu.VMEM((slot_count, Q // group, batch, group * S * U), f32),
            pltpu.VMEM((slot_count, Q // group, batch, group * S * U), f32),
            pltpu.VMEM((slot_count, Q // group, group * S * U), f32),
            pltpu.VMEM((slot_count, Q // group, group * S * U), f32),
            pltpu.VMEM((2, n_phase, C, Q // group, batch, group * S * U), f32),
            sems((max(1, len(masks)),)),
            sems((max(1, len(masks)),)),
            sems((2 * near_count,)),
            sems((2 * near_count,)),
            sems((2 * near_count,)),
            sems((2 * near_count,)),
            sems((edge_count,)),
            sems((edge_count,)),
        ],
        compiler_params=pltpu.CompilerParams(
            collective_id=0, has_side_effects=True, vmem_limit_bytes=52 * 1024 * 1024
        ),
    )(coef, leave, spots, state_values, band)


def solution(mesh):
    placed = (
        P(("groups", "level"), "src", "phase", None, None),
        P("groups", None),
        P("groups", None, None),
        P("groups"),
        P("groups", None),
        P("groups", None),
        P("groups", None),
        P("groups"),
    )
    axes = mesh.shape
    return jax.shard_map(
        functools.partial(body, axes["level"], axes["src"], axes["phase"]),
        mesh=mesh,
        in_specs=placed,
        out_specs=P(("groups", "level"), "src", "phase", None, None),
        check_vma=False,
    )
```

time: 396 us -> 139 us (0.35)
  the two profiles are of different devices: /device:TPU:0 before, /device:TPU:31 now
where the time goes in v1:
time: 139 us
  Pallas kernels  112 us (81%)
  local copies, waits for them, and re-layouts  12.2 us (9%)
  other arithmetic  6.86 us (5%)
  matrix products  5.35 us (4%)
  between operations  2.6 us (2%)
    pallas_call x1, Pallas kernels, body(): pl.pallas_call(functools.partial(kernel, sizes), out_shape=jax.ShapeDtype...  112 us
    dot_general x1, matrix products, body(): jnp.einsum('bpq,bvw->qvpw', tables, hot, precision=lax.Precision.HIGHEST)  5.35 us
    unnamed x6, local copies, waits for them, and re-layouts  5.33 us
    reshape x1, local copies, waits for them, and re-layouts, body(): band = band.reshape(Q * batch, phases * 2 * batch)  3.74 us

profile of v1, /device:TPU:31, one launch (start us, length us, event | category | flops | bytes accessed | tf_op | source)
XLA Modules:
  0.0 138.7 jit_solution(13812431051307761776)
XLA Ops:
  0.0 1.1 reduce_sum.75
  1.1 0.8 fusion.11
  2.0 0.7 broadcast_add_fusion
  2.6 1.4 %fusion.17 = (f32[1]{0:T(128)}, f32[1]{0:T(128)}) fusion(f32[2]{0:T(128)} %param.13), kind=kLoop, calls=%fused_computation.50 | loop fusion | bytes 16 | tf_op jit(solution)/shard_map/slice | solution.py:330
  4.0 0.1 copy.22
  4.1 0.7 compare_convert_fusion
  4.8 1.0 slice_reduce_fusion.1
  5.9 0.6 fusion.16
  6.5 0.8 copy.20
  7.3 0.2 select_reduce_fusion
  7.5 0.7 pad_add_fusion
  8.3 0.1 multiply_reduce_fusion
  8.6 0.8 copy.17
  9.4 0.6 fusion.15
  12.7 0.7 broadcast_divide_fusion
  13.3 0.2 fusion.14
  13.5 0.1 copy.19
  13.6 0.1 copy.18
  13.8 0.1 stack.3
  14.0 1.1 copy.23
  15.2 5.3 %convolution_bitcast_fusion = f32[16,16,32,32]{3,2,1,0:T(8,128)} fusion(f32[17,16,32,1]{2,0,1,3:T(8,128)S(1)} %copy-done, s32[]{:T(128)S(6)} %select_n.42, f32[17,32,16]{1,0,2:T(8,128)S(1)} %fusion.1), kind=kOutput, calls=%fused_computation | convolution fusion | flops 53486080 | bytes 1118212 | tf_op jit(solution)/shard_map/bpq,bvw->qvpw/dot_general | solution.py:338
  20.6 3.7 %reshape.80.band_ref = f32[256,1024]{1,0:T(8,128)S(1)} reshape(f32[16,16,32,32]{3,2,1,0:T(8,128)} %convolution_bitcast_fusion) | data formatting | bytes 2097152 | tf_op jit(solution)/shard_map/reshape | solution.py:339
  24.3 111.7 %shard_map.100 = f32[3,4,16,16,128]{4,3,2,1,0:T(8,128)} custom-call(f32[38]{0:T(128)S(1)} %pad_maximum_fusion.coef, f32[16]{0:T(128)S(1)} %dynamic-slice_divide_fusion.leave, s32[24]{0:T(128)S(1)} %reshape.79.spots, f32[3,4,16,16,128]{4,3,2,1,0:T(8,128)} %x_ref.1, f32[256,1024]{1,0:T(8,128)S(1)} %reshape.80.band_ref), custom_call_target="tpu_custom_call" | custom-call | tf_op jit(solution)/shard_map/pallas_call | solution.py:383
  136.1 2.7 %copy.26 = f32[3,4,16,16,128]{4,3,2,1,0:T(8,128)} copy(f32[3,4,16,16,128]{4,3,2,1,0:T(8,128)} %shard_map.100) | data formatting | bytes 3145728
  (16 shorter events, 0.7 us)
Async XLA Ops:
  0.0 15.2 %copy-start = (f32[17,16,32,1]{2,0,1,3:T(8,128)S(1)}, f32[17,16,32,1]{2,0,1,3:T(8,128)}, u32[]{:S(2)}) copy-start(f32[17,16,32,1]{2,0,1,3:T(8,128)} %constant.64) | copy-start | bytes 104452

commit v2 on v1

v2 whole, which is shorter than its diff:
```python
import functools

import jax
import jax.numpy as jnp
from jax import lax
from jax.experimental import pallas as pl
from jax.experimental.pallas import tpu as pltpu
from jax.sharding import PartitionSpec as P

SOURCES = 3
MESH = pl.DeviceIdType.MESH


def split(values):
    high = values.astype(jnp.bfloat16)
    low = (values - high.astype(jnp.float32)).astype(jnp.bfloat16)
    return high, low


def kernel(
    sizes,
    service,
    sources,
    levels,
    routes,
    owner,
    x_ref,
    phase_rates,
    batch_rates,
    out_ref,
    far,
    far_edge,
    far_left,
    near,
    mixed,
    high,
    low,
    conv,
    base,
    band,
    band_cat,
    leave,
    edge_one,
    edge_two,
    rim_one,
    rim_two,
    rim_mixed,
    picks,
    left_own,
    far_send,
    far_recv,
    far_edge_send,
    far_edge_recv,
    far_left_send,
    far_left_recv,
    near_send,
    near_recv,
    pick_send,
    pick_recv,
    edge_send,
    edge_recv,
):
    n_level, n_phase, masks, local_bits, cross = sizes
    singles = len(cross)
    C, S, Q, U, V = x_ref.shape
    SU = S * U
    CSU = C * SU
    B = rim_one.shape[-2]
    G = rim_one.shape[-1] // SU
    groups = Q // G
    lanes = G * SU
    phases = n_phase * Q
    wide = 2 * B
    low_at = groups * B
    up_at = low_at + C * S * Q
    bot_at = up_at + C * S * Q
    bot_rows = (edge_one.shape[1] - bot_at) // C
    level, src, phase = (lax.axis_index(n) for n in ("level", "src", "phase"))
    cores = [{"phase": lax.rem(phase + r, n_phase)} for r in range(1, n_phase)]
    fars = [{"src": jnp.bitwise_xor(src, m)} for m in masks]
    sides = ((1, level < n_level - 1, level > 0), (-1, level > 0, level < n_level - 1))

    barrier = pltpu.get_barrier_semaphore()
    for device in cores + fars:
        pl.semaphore_signal(barrier, inc=1, device_id=device, device_id_type=MESH)
    for toward, ahead, behind in sides:

        @pl.when(ahead)
        def _():
            pl.semaphore_signal(
                barrier, inc=1, device_id={"level": level + toward}, device_id_type=MESH
            )

    beside = (level > 0).astype(jnp.int32) + (level < n_level - 1).astype(jnp.int32)
    pl.semaphore_wait(barrier, len(cores) + len(fars) + beside)

    def make(source, target, sems, index, device):
        return pltpu.make_async_remote_copy(
            src_ref=source,
            dst_ref=target,
            send_sem=sems[0].at[index],
            recv_sem=sems[1].at[index],
            device_id=device,
            device_id_type=MESH,
        )

    def send(*parts):
        copy = make(*parts)
        copy.start()
        return copy

    def hop(step, edge, way, h, act):
        toward, ahead, _ = sides[way]
        block = level - toward * h
        index = (step * 2 + way) * (n_level - 1) + h
        held = jnp.logical_and(block >= 0, block < n_level)

        @pl.when(jnp.logical_and(held, ahead))
        def _():
            part = edge.at[block]
            device = {"level": level + toward}
            act(make(part, part, (edge_send, edge_recv), index, device))

    def start_hop(step, edge, h):
        for way in range(2):
            hop(step, edge, way, h, lambda copy: copy.start())

    def end_hop(step, edge, h):
        for way in range(2):
            toward = sides[way][0]
            block = level - toward * (h + 1)
            index = (step * 2 + way) * (n_level - 1) + h

            @pl.when(jnp.logical_and(block >= 0, block < n_level))
            def _():
                part = edge.at[block]
                device = {"level": level - toward}
                make(part, part, (edge_send, edge_recv), index, device).wait_recv()

            if h < n_level - 2:
                hop(step, edge, way, h + 1, lambda copy: copy.start())

    def end_sends(step, edge):
        for h in range(n_level - 1):
            for way in range(2):
                hop(step, edge, way, h, lambda copy: copy.wait_send())

    near_sems = (near_send, near_recv)
    x_near = [
        send(x_ref, near.at[0, r], near_sems, r, device) for r, device in enumerate(cores)
    ]

    tile_count = owner.shape[0]
    spots = []
    count = jnp.int32(0)
    for c in range(C):
        tile, filled = jnp.int32(0), jnp.int32(0)
        for t in range(tile_count):
            here = owner[t] == level * C + c
            tile = jnp.where(here, t, tile)
            filled = jnp.where(here, 1, filled)
        places = []
        for n in range(5):
            route = routes[tile, n]
            slot = owner[jnp.maximum(route, 0)]
            at = lax.div(slot, jnp.int32(C))
            places.append((route >= 0, at, slot - at * C))
        spots.append((places, levels[tile, 0], levels[tile, 1], filled))
        count = count + filled
    last = jnp.maximum(count - 1, 0)

    def turn(field, i, g):
        return field[:, :, i * G + g].reshape(CSU, V).T

    def put(first, i, g, turned):
        top, rest = split(turned)
        high[first + i * G + g, B:, :] = top
        low[first + i * G + g, B:, :] = rest

    def keep_rims(rim, i, turned):
        for c in range(C):
            part = slice(c * SU, (c + 1) * SU)
            rim[c, i] = jnp.concatenate([t[V - B :, part] for t in turned], axis=1)

    def keep_bots(edge, i, turned):
        for c in range(C):
            part = slice(c * SU, (c + 1) * SU)
            edge[level, pl.ds(bot_at + c * bot_rows + i, 1), :] = jnp.concatenate(
                [t[0:1, part] for t in turned], axis=1
            )

    def keep_rows(edge, rim, field):
        for c in range(C):
            for s in range(S):
                at = (c * S + s) * Q
                edge[level, low_at + at : low_at + at + Q, :] = field[c, s, :, U - 1, :]
                edge[level, up_at + at : up_at + at + Q, :] = field[c, s, :, 0, :]
        edge[level, 0:low_at, :] = rim[last].reshape(low_at, lanes)
        if bot_rows > groups:
            for c in range(C):
                at = bot_at + c * bot_rows
                edge[level, at + groups : at + bot_rows, :] = jnp.zeros(
                    (bot_rows - groups, lanes), jnp.float32
                )

    def turn_own(i, carry):
        turned = [turn(x_ref, i, g) for g in range(G)]
        for g in range(G):
            put(0, i, g, turned[g])
        keep_rims(rim_one, i, turned)
        keep_bots(edge_one, i, turned)
        return carry

    lax.fori_loop(0, groups, turn_own, 0)
    keep_rows(edge_one, rim_one, x_ref)
    start_hop(0, edge_one, 0)
    edge_copies = [
        send(edge_one.at[level], far_edge.at[m], (far_edge_send, far_edge_recv), m, device)
        for m, device in enumerate(fars[:singles])
    ]
    far_copies = [
        [
            send(x_ref.at[:, s], far.at[m, :, s], (far_send, far_recv), m * S + s, device)
            for m, device in enumerate(fars)
        ]
        for s in range(S)
    ]

    across = lax.broadcasted_iota(jnp.int32, (phases, phases), 0) == lax.broadcasted_iota(
        jnp.int32, (phases, phases), 1
    )
    moving = jnp.where(across, 0.0, phase_rates[...])
    sums = moving
    for b in range(B):
        sums = sums + batch_rates[b]
    leaving = jnp.sum(sums, axis=1, keepdims=True)
    uniform = jnp.max(leaving) + service[0] + service[1]
    for k in range(SOURCES):
        uniform = uniform + jnp.maximum(sources[k, 2] + sources[k, 1], sources[k, 0])
    inverse = jnp.max(1.0 / jnp.full((8, 128), uniform, jnp.float32))
    leave[...] = jnp.broadcast_to(leaving * inverse, leave.shape)
    serve_one, serve_two = service[0] * inverse, service[1] * inverse
    turn_on = [sources[k, 0] * inverse for k in range(SOURCES)]
    turn_off = [sources[k, 1] * inverse for k in range(SOURCES)]
    arrive = [sources[k, 2] * inverse for k in range(SOURCES)]
    bit = {k: ((src >> (k - local_bits)) & 1) == 1 for k in cross}
    inflow = {k: jnp.where(bit[k], turn_on[k], turn_off[k]) for k in cross}
    outflow = {k: jnp.where(bit[k], turn_off[k], turn_on[k]) for k in cross}
    more_feed = {k: jnp.where(bit[k], -arrive[k], arrive[k]) for k in cross}
    feed, total_out = [], []
    for s in range(S):
        f = o = jnp.float32(0.0)
        for k in range(SOURCES):
            if k in cross:
                f = f + jnp.where(bit[k], arrive[k], 0.0)
                o = o + outflow[k]
            elif s >> k & 1:
                f, o = f + arrive[k], o + turn_off[k]
            else:
                o = o + turn_on[k]
        feed.append(f)
        total_out.append(o)
    twice = [2.0 * inflow[k] for k in cross]
    shift_in = [inflow[k] * more_feed[k] for k in cross]
    stay_in = [-inflow[k] * (more_feed[k] + inflow[k] - outflow[k]) for k in cross]
    back_in = jnp.float32(0.0)
    for k in cross:
        back_in = back_in + inflow[k] * outflow[k]
    pair_in = [
        2.0 * inflow[a] * inflow[b] for i, a in enumerate(cross) for b in cross[i + 1 :]
    ]

    base[...] = jnp.zeros(base.shape, jnp.float32)
    for r in range(n_phase):
        rank = lax.rem(phase + r, n_phase)
        at = pl.ds(pl.multiple_of(rank * Q, Q), Q)
        for w in range(B):
            base[pl.ds(r * Q * wide + w, Q, stride=wide), 0:phases] = (
                batch_rates[B - 1 - w, at, :] * inverse
            )
        row = lax.broadcasted_iota(jnp.int32, (Q, phases), 0) + rank * Q
        column = lax.broadcasted_iota(jnp.int32, (Q, phases), 1)
        base[pl.ds(r * Q * wide + B, Q, stride=wide), 0:phases] = (
            jnp.where(row == column, 0.0, phase_rates[at, :]) * inverse
        )
    out_rows = base[...].T
    base_two = jnp.zeros((Q, phases * wide), jnp.float32)
    for r in range(n_phase):
        base_two = jnp.where(phase == r, out_rows[r * Q : (r + 1) * Q], base_two)
    for v in range(B):
        band[:, v, :] = pltpu.roll(base_two, v, 1) if v else base_two
    M = Q * B
    band_high, band_low = split(band[...].reshape(M, phases * wide))
    band_cat[0:M, :] = band_high
    band_cat[M:, :] = band_low

    def multiply(v, carry):
        window = pl.ds(pl.multiple_of(v * B, B), wide)
        top = high[:, window, :].reshape(phases * wide, CSU)
        rest = low[:, window, :].reshape(phases * wide, CSU)
        both = jnp.dot(band_cat[...], top, preferred_element_type=jnp.float32)
        third = jnp.dot(band_cat[0:M, :], rest, preferred_element_type=jnp.float32)
        total = both[0:M] + (both[M:] + third)
        conv[:, pl.ds(pl.multiple_of(v * B, B), B), :] = total.reshape(Q, B, CSU)
        return carry

    def turn_near(step):
        for r in range(n_phase - 1):

            def one(i, carry):
                for g in range(G):
                    put((r + 1) * Q, i, g, turn(near.at[step, r], i, g))
                return carry

            lax.fori_loop(0, groups, one, 0)

    def spread(i, first, values):
        for g in range(G):
            whole = jnp.concatenate([v[:, g * SU : (g + 1) * SU] for v in values], axis=1)
            top, rest = split(whole)
            high[first + i * G + g, 0:B, :] = top
            low[first + i * G + g, 0:B, :] = rest

    def take_rims(step, edge, rim):
        def pick(i, carry):
            values = []
            for c in range(C):
                there, at, _ = spots[c][0][0]
                if c == 0:
                    found = edge[at, pl.ds(pl.multiple_of(i * B, B), B), :]
                else:
                    found = rim[c - 1, i]
                value = jnp.where(there, found, 0.0)
                picks[step, 0, c, i] = value
                values.append(value)
            spread(i, 0, values)
            return carry

        lax.fori_loop(0, groups, pick, 0)
        copies = [
            send(
                picks.at[step, 0],
                picks.at[step, r + 1],
                (pick_send, pick_recv),
                step * (n_phase - 1) + r,
                device,
            )
            for r, device in enumerate(cores)
        ]
        for r, copy in enumerate(copies):
            copy.wait_recv()

            def take(i, carry):
                spread(i, (r + 1) * Q, [picks[step, r + 1, c, i] for c in range(C)])
                return carry

            lax.fori_loop(0, groups, take, 0)
        multiply(0, 0)
        return copies

    def add_above(edge):
        def one(i, carry):
            lane = lax.broadcasted_iota(jnp.int32, (8, lanes), 1)
            values = []
            for c in range(C):
                rolled = []
                for n, amount in ((1, 1), (4, lanes - (U - 1))):
                    there, at, slot = spots[c][0][n]
                    found = edge[at, pl.ds(bot_at + slot * bot_rows + i, 1), :]
                    found = jnp.broadcast_to(jnp.where(there, found, 0.0), (8, lanes))
                    rolled.append(pltpu.roll(found, amount, 1))
                values.append(jnp.where(lane % U == 0, rolled[1], rolled[0]))
            for g in range(G):
                whole = jnp.concatenate([v[:, g * SU : (g + 1) * SU] for v in values], axis=1)
                q = i * G + g
                conv[q, V - 1 : V, :] = conv[q, V - 1 : V, :] + serve_one * whole[0:1]
            return carry

        lax.fori_loop(0, groups, one, 0)

    def beside_row(edge, place, first, s, q):
        there, at, slot = place
        found = edge[at, pl.ds(first + (slot * S + s) * Q + q, 1), :]
        return jnp.where(there, found, 0.0)

    def combine(step, edge, field):
        def one(q, carry):
            back = conv[q].T
            line = lax.broadcasted_iota(jnp.int32, (U, V), 0)
            lane = lax.broadcasted_iota(jnp.int32, (U, V), 1)
            gone_here = leave[pl.ds(phase * Q + q, 1), :]

            for c in range(C):
                places, level_one, level_two, filled = spots[c]
                gone = (
                    gone_here
                    + jnp.where(level_one * V + lane > 0, serve_one, 0.0)
                    + jnp.where(level_two * U + line > 0, serve_two, 0.0)
                )
                blocks = [field[c, s, q] for s in range(S)]
                for s in range(S):
                    here = blocks[s]
                    block = c * S + s
                    value = here + back[block * U : (block + 1) * U]
                    left = jnp.broadcast_to(beside_row(edge, places[2], low_at, s, q), (U, V))
                    right = jnp.broadcast_to(beside_row(edge, places[3], up_at, s, q), (U, V))
                    before = jnp.where(line == 0, left, pltpu.roll(here, 1, 0))
                    after = jnp.where(line == U - 1, right, pltpu.roll(here, U - 1, 0))
                    moved = jnp.where(lane == V - 1, 0.0, pltpu.roll(before, V - 1, 1))
                    value = value + serve_one * moved + serve_two * after + feed[s] * before
                    value = value - (gone + (feed[s] + total_out[s])) * here
                    for k in range(local_bits):
                        rate = turn_on[k] if s >> k & 1 else turn_off[k]
                        value = value + rate * blocks[s ^ (1 << k)]
                    if step == 0:
                        mixed[c, s, q] = value
                    else:
                        if singles:
                            shifted = jnp.zeros((U, V), jnp.float32)
                            first = jnp.zeros((1, V), jnp.float32)
                            for k in range(singles):
                                other = far[k, c, s, q]
                                shifted = shifted + shift_in[k] * other
                                first = first + shift_in[k] * (
                                    far_left[k, c, pl.ds(s * Q + q, 1), :]
                                )
                                value = value + stay_in[k] * other
                            shifted = jnp.where(
                                line == 0,
                                jnp.broadcast_to(first, (U, V)),
                                pltpu.roll(shifted, 1, 0),
                            )
                            value = value + shifted + back_in * x_ref[c, s, q]
                        for k in range(singles, len(masks)):
                            value = value + pair_in[k - singles] * far[k, c, s, q]
                        out_ref[c, s, q] = jnp.where(filled > 0, value, 0.0)
            return carry

        lax.fori_loop(0, Q, one, 0)

    for copy in x_near:
        copy.wait_recv()
    turn_near(0)
    if n_level > 1:
        end_hop(0, edge_one, 0)
    lax.fori_loop(1, V // B, multiply, 0)
    for h in range(1, n_level - 1):
        end_hop(0, edge_one, h)
    pick_copies = take_rims(0, edge_one, rim_one)
    add_above(edge_one)

    def keep_left(q, carry):
        for c in range(C):
            for s in range(S):
                left_own[c, pl.ds(s * Q + q, 1), :] = beside_row(
                    edge_one, spots[c][0][2], low_at, s, q
                )
        return carry

    lax.fori_loop(0, Q, keep_left, 0)
    left_copies = [
        send(left_own, far_left.at[m], (far_left_send, far_left_recv), m, device)
        for m, device in enumerate(fars[:singles])
    ]
    combine(0, edge_one, x_ref)

    def turn_edges(i, carry):
        turned = [turn(mixed, i, g) for g in range(G)]
        keep_rims(rim_mixed, i, turned)
        keep_bots(edge_two, i, turned)
        return carry

    lax.fori_loop(0, groups, turn_edges, 0)
    keep_rows(edge_two, rim_mixed, mixed)
    for k, copy in enumerate(edge_copies):
        copy.wait_recv()
        edge_two[level] = edge_two[level] + twice[k] * far_edge[k]
    start_hop(1, edge_two, 0)
    mixed_near = []
    for s in range(S):
        for m, copy in enumerate(far_copies[s]):
            copy.wait_recv()
        for c in range(C):

            def add(q, carry):
                value = mixed[c, s, q]
                for k in range(singles):
                    value = value + twice[k] * far[k, c, s, q]
                mixed[c, s, q] = value
                return carry

            lax.fori_loop(0, Q, add, 0)
        for r, device in enumerate(cores):
            index = (n_phase - 1) * (1 + s) + r
            mixed_near.append(
                send(mixed.at[:, s], near.at[1, r, :, s], near_sems, index, device)
            )
        if s == 0 and n_level > 1:
            end_hop(1, edge_two, 0)

    def turn_mixed(i, carry):
        turned = [turn(mixed, i, g) for g in range(G)]
        for g in range(G):
            put(0, i, g, turned[g])
        keep_rims(rim_two, i, turned)
        return carry

    lax.fori_loop(0, groups, turn_mixed, 0)
    if n_level > 2:
        end_hop(1, edge_two, 1)
    for copy in mixed_near:
        copy.wait_recv()
    turn_near(1)
    lax.fori_loop(1, V // B, multiply, 0)
    for h in range(2, n_level - 1):
        end_hop(1, edge_two, h)
    pick_copies += take_rims(1, edge_two, rim_two)
    add_above(edge_two)
    for copy in left_copies:
        copy.wait_recv()
    combine(1, edge_two, mixed)

    for copy in x_near + mixed_near + pick_copies + left_copies + edge_copies:
        copy.wait_send()
    for copies in far_copies:
        for copy in copies:
            copy.wait_send()
    end_sends(0, edge_one)
    end_sends(1, edge_two)


def body(
    n_level,
    n_phase,
    state_values,
    phase_rates,
    batch_rates,
    service_rates,
    source_rates,
    tile_levels,
    routes,
    tile_owner,
):
    C, S, Q, U, V = state_values.shape
    phases = phase_rates.shape[0]
    batch = batch_rates.shape[0]
    local_bits = S.bit_length() - 1
    cross = list(range(local_bits, SOURCES))
    masks = [1 << (k - local_bits) for k in cross]
    masks += [masks[i] | masks[j] for i in range(len(cross)) for j in range(i + 1, len(cross))]
    group = min(Q, max(1, 128 // (S * U)))
    lanes = group * S * U
    groups = Q // group
    edge_rows = groups * batch + 2 * C * S * Q + C * (-(-groups // 8) * 8)
    f32, bf16 = jnp.float32, jnp.bfloat16
    vmem = pl.BlockSpec(memory_space=pltpu.VMEM)
    smem = pl.BlockSpec(memory_space=pltpu.SMEM)
    singles, fars, cores = max(1, len(cross)), max(1, len(masks)), max(1, n_phase - 1)
    counts = [fars * S, singles, singles, cores * (1 + S), 2 * cores, max(1, 4 * (n_level - 1))]
    shapes = [
        ((fars,) + state_values.shape, f32),
        ((singles, edge_rows, lanes), f32),
        ((singles, C, S * Q, V), f32),
        ((2, cores) + state_values.shape, f32),
        (state_values.shape, f32),
        ((phases, batch + V, C * S * U), bf16),
        ((phases, batch + V, C * S * U), bf16),
        ((Q, V, C * S * U), f32),
        ((phases * 2 * batch, 128), f32),
        ((Q, batch, phases * 2 * batch), f32),
        ((2 * Q * batch, phases * 2 * batch), bf16),
        ((phases, V), f32),
        ((n_level, edge_rows, lanes), f32),
        ((n_level, edge_rows, lanes), f32),
        ((C, groups, batch, lanes), f32),
        ((C, groups, batch, lanes), f32),
        ((C, groups, batch, lanes), f32),
        ((2, n_phase, C, groups, batch, lanes), f32),
        ((C, S * Q, V), f32),
    ]
    return pl.pallas_call(
        functools.partial(kernel, (n_level, n_phase, masks, local_bits, cross)),
        out_shape=jax.ShapeDtypeStruct(state_values.shape, f32),
        in_specs=[smem] * 5 + [vmem] * 3,
        out_specs=vmem,
        scratch_shapes=[pltpu.VMEM(*shape) for shape in shapes]
        + [pltpu.SemaphoreType.DMA((n,)) for n in counts for _ in range(2)],
        compiler_params=pltpu.CompilerParams(
            collective_id=0, has_side_effects=True, vmem_limit_bytes=52 * 1024 * 1024
        ),
    )(
        service_rates,
        source_rates,
        tile_levels,
        routes,
        tile_owner,
        state_values,
        phase_rates,
        batch_rates,
    )


def solution(mesh):
    placed = (
        P(("groups", "level"), "src", "phase", None, None),
        P("groups", None),
        P("groups", None, None),
        P("groups"),
        P("groups", None),
        P("groups", None),
        P("groups", None),
        P("groups"),
    )
    axes = mesh.shape
    return jax.shard_map(
        functools.partial(body, axes["level"], axes["phase"]),
        mesh=mesh,
        in_specs=placed,
        out_specs=P(("groups", "level"), "src", "phase", None, None),
        check_vma=False,
    )
```

time: 139 us -> 72.3 us (0.52)
  the two profiles are of different devices: /device:TPU:31 before, /device:TPU:0 now
where the time goes in v2:
time: 72.3 us; the launch traced here: 71 us
  Pallas kernels  64.7 us (89%)
  local copies, waits for them, and re-layouts  6.24 us (9%)
    pallas_call x1, Pallas kernels, body(): pl.pallas_call(functools.partial(kernel, (n_level, n_phase, masks, local_...  64.7 us
    unnamed x14, local copies, waits for them, and re-layouts  6.24 us

profile of v2, /device:TPU:0, one launch (start us, length us, event | category | flops | bytes accessed | tf_op | source)
XLA Modules:
  0.0 71.0 jit_solution(11723533975833783093)
XLA Ops:
  0.0 0.8 %copy.9.levels = s32[8,2]{1,0:T(8,128)S(1)} copy(s32[8,2]{0,1:T(2,128)} %param.13) | data formatting | bytes 128 | tf_op args[5]
  0.8 0.0 copy-start
  0.8 0.9 %copy-done = f32[16,32,32]{2,1,0:T(8,128)S(1)} copy-done((f32[16,32,32]{2,1,0:T(8,128)S(1)}, f32[16,32,32]{2,1,0:T(8,128)}, u32[]{:S(2)}) %copy-start) | copy-done | bytes 65560
  1.7 0.0 copy-start.1
  1.7 0.7 %copy-done.1 = f32[32,32]{1,0:T(8,128)S(1)} copy-done((f32[32,32]{1,0:T(8,128)S(1)}, f32[32,32]{1,0:T(8,128)}, u32[]{:S(2)}) %copy-start.1) | copy-done | bytes 4120
  2.4 0.0 copy-start.2
  2.4 0.7 copy-done.2
  3.1 0.0 copy-start.3
  3.1 0.7 copy-done.3
  3.8 0.0 copy-start.4
  3.8 0.7 copy-done.4
  4.4 0.0 copy-start.5
  4.4 0.7 copy-done.5
  5.1 64.7 %shard_map.82 = f32[3,4,16,16,128]{4,3,2,1,0:T(8,128)S(1)} custom-call(f32[2]{0:T(128)S(1)} %copy-done.4, f32[3,3]{1,0:T(4,128)S(1)} %copy-done.3, s32[8,2]{1,0:T(8,128)S(1)} %copy.9.levels, s32[8,5]{1,0:T(8,128)S(1)} %copy-done.2, s32[8]{0:T(128)S(1)} %copy-done.5, f32[3,4,16,16,128]{4,3,2,1,0:T(8,128)} %x_ref.1, f32[32,32]{1,0:T(8,128)S(1)} %copy-done.1, ...), custom_call_target="tpu_custom_call" | custom-call | tf_op jit(solution)/shard_map/pallas_call | solution.py:581
  69.8 1.1 %copy.11 = f32[3,4,16,16,128]{4,3,2,1,0:T(8,128)} copy(f32[3,4,16,16,128]{4,3,2,1,0:T(8,128)S(1)} %shard_map.82) | data formatting | bytes 3145728
Async XLA Ops:
  0.8 0.9 %copy-start = (f32[16,32,32]{2,1,0:T(8,128)S(1)}, f32[16,32,32]{2,1,0:T(8,128)}, u32[]{:S(2)}) copy-start(f32[16,32,32]{2,1,0:T(8,128)} %batch_rates.1) | copy-start | bytes 196612
  1.7 0.7 %copy-start.1 = (f32[32,32]{1,0:T(8,128)S(1)}, f32[32,32]{1,0:T(8,128)}, u32[]{:S(2)}) copy-start(f32[32,32]{1,0:T(8,128)} %phase_rates.1) | copy-start | bytes 12292
  2.4 0.7 copy-start.2
  3.1 0.7 copy-start.3
  3.8 0.7 copy-start.4
  4.4 0.7 copy-start.5

commit v3 on v2

--- a/solution.py
+++ b/solution.py
@@ -19,6 +19,22 @@
 
 def kernel(
     sizes,
+    *refs,
+):
+    operands, out_ref, held, fetch, rest = refs[:8], refs[8], refs[9:17], refs[17], refs[18:]
+    fetches = [
+        pltpu.make_async_copy(operand, ref, fetch.at[n])
+        for n, (operand, ref) in enumerate(zip(operands, held))
+    ]
+    for copy in fetches:
+        copy.start()
+    steps(sizes, fetches, operands[5], *held, out_ref, *rest)
+
+
+def steps(
+    sizes,
+    fetches,
+    x_hbm,
     service,
     sources,
     levels,
@@ -71,10 +87,12 @@
     lanes = G * SU
     phases = n_phase * Q
     wide = 2 * B
-    low_at = groups * B
-    up_at = low_at + C * S * Q
-    bot_at = up_at + C * S * Q
+    low_at = 0
+    up_at = C * S * Q
+    rim_at = 2 * C * S * Q
+    bot_at = rim_at + groups * B
     bot_rows = (edge_one.shape[1] - bot_at) // C
+    parts = (pl.ds(0, rim_at), pl.ds(rim_at, edge_one.shape[1] - rim_at))
     level, src, phase = (lax.axis_index(n) for n in ("level", "src", "phase"))
     cores = [{"phase": lax.rem(phase + r, n_phase)} for r in range(1, n_phase)]
     fars = [{"src": jnp.bitwise_xor(src, m)} for m in masks]
@@ -109,46 +127,53 @@
         copy.start()
         return copy
 
-    def hop(step, edge, way, h, act):
+    def edge_copy(step, edge, part, way, h, block, toward):
+        index = ((step * 2 + part) * 2 + way) * (n_level - 1) + h
+        piece = edge.at[block, parts[part]]
+        return make(piece, piece, (edge_send, edge_recv), index, {"level": level + toward})
+
+    def hop(step, edge, part, way, h, act):
         toward, ahead, _ = sides[way]
         block = level - toward * h
-        index = (step * 2 + way) * (n_level - 1) + h
         held = jnp.logical_and(block >= 0, block < n_level)
 
         @pl.when(jnp.logical_and(held, ahead))
         def _():
-            part = edge.at[block]
-            device = {"level": level + toward}
-            act(make(part, part, (edge_send, edge_recv), index, device))
-
-    def start_hop(step, edge, h):
+            act(edge_copy(step, edge, part, way, h, block, toward))
+
+    def start_hop(step, edge, part):
         for way in range(2):
-            hop(step, edge, way, h, lambda copy: copy.start())
-
-    def end_hop(step, edge, h):
+            hop(step, edge, part, way, 0, lambda copy: copy.start())
+
+    def end_hop(step, edge, part, h):
         for way in range(2):
             toward = sides[way][0]
             block = level - toward * (h + 1)
-            index = (step * 2 + way) * (n_level - 1) + h
 
             @pl.when(jnp.logical_and(block >= 0, block < n_level))
             def _():
-                part = edge.at[block]
-                device = {"level": level - toward}
-                make(part, part, (edge_send, edge_recv), index, device).wait_recv()
+                edge_copy(step, edge, part, way, h, block, -toward).wait_recv()
 
             if h < n_level - 2:
-                hop(step, edge, way, h + 1, lambda copy: copy.start())
+                hop(step, edge, part, way, h + 1, lambda copy: copy.start())
+
+    def end_hops(step, edge, first, end):
+        for h in range(first, min(end, n_level - 1)):
+            for part in range(2):
+                end_hop(step, edge, part, h)
 
     def end_sends(step, edge):
-        for h in range(n_level - 1):
-            for way in range(2):
-                hop(step, edge, way, h, lambda copy: copy.wait_send())
+        for part in range(2):
+            for h in range(n_level - 1):
+                for way in range(2):
+                    hop(step, edge, part, way, h, lambda copy: copy.wait_send())
 
     near_sems = (near_send, near_recv)
     x_near = [
-        send(x_ref, near.at[0, r], near_sems, r, device) for r, device in enumerate(cores)
+        send(x_hbm, near.at[0, r], near_sems, r, device) for r, device in enumerate(cores)
     ]
+    for copy in fetches:
+        copy.wait()
 
     tile_count = owner.shape[0]
     spots = []
@@ -189,13 +214,15 @@
                 [t[0:1, part] for t in turned], axis=1
             )
 
-    def keep_rows(edge, rim, field):
+    def keep_rows(edge, field):
         for c in range(C):
             for s in range(S):
                 at = (c * S + s) * Q
                 edge[level, low_at + at : low_at + at + Q, :] = field[c, s, :, U - 1, :]
                 edge[level, up_at + at : up_at + at + Q, :] = field[c, s, :, 0, :]
-        edge[level, 0:low_at, :] = rim[last].reshape(low_at, lanes)
+
+    def keep_last(edge, rim):
+        edge[level, rim_at:bot_at, :] = rim[last].reshape(bot_at - rim_at, lanes)
         if bot_rows > groups:
             for c in range(C):
                 at = bot_at + c * bot_rows
@@ -211,16 +238,18 @@
         keep_bots(edge_one, i, turned)
         return carry
 
+    keep_rows(edge_one, x_ref)
+    start_hop(0, edge_one, 0)
     lax.fori_loop(0, groups, turn_own, 0)
-    keep_rows(edge_one, rim_one, x_ref)
-    start_hop(0, edge_one, 0)
+    keep_last(edge_one, rim_one)
+    start_hop(0, edge_one, 1)
     edge_copies = [
         send(edge_one.at[level], far_edge.at[m], (far_edge_send, far_edge_recv), m, device)
         for m, device in enumerate(fars[:singles])
     ]
     far_copies = [
         [
-            send(x_ref.at[:, s], far.at[m, :, s], (far_send, far_recv), m * S + s, device)
+            send(x_hbm.at[:, s], far.at[m, :, s], (far_send, far_recv), m * S + s, device)
             for m, device in enumerate(fars)
         ]
         for s in range(S)
@@ -327,7 +356,7 @@
             for c in range(C):
                 there, at, _ = spots[c][0][0]
                 if c == 0:
-                    found = edge[at, pl.ds(pl.multiple_of(i * B, B), B), :]
+                    found = edge[at, pl.ds(pl.multiple_of(rim_at + i * B, 8), B), :]
                 else:
                     found = rim[c - 1, i]
                 value = jnp.where(there, found, 0.0)
@@ -378,20 +407,18 @@
 
         lax.fori_loop(0, groups, one, 0)
 
-    def beside_row(edge, place, first, s, q):
+    def beside(edge, place, first, s):
         there, at, slot = place
-        found = edge[at, pl.ds(first + (slot * S + s) * Q + q, 1), :]
-        return jnp.where(there, found, 0.0)
-
-    def combine(step, edge, field):
+        return jnp.where(there, edge[at, pl.ds(first + (slot * S + s) * Q, Q), :], 0.0)
+
+    def combine(step, field, result):
         def one(q, carry):
-            back = conv[q].T
             line = lax.broadcasted_iota(jnp.int32, (U, V), 0)
             lane = lax.broadcasted_iota(jnp.int32, (U, V), 1)
             gone_here = leave[pl.ds(phase * Q + q, 1), :]
 
             for c in range(C):
-                places, level_one, level_two, filled = spots[c]
+                _, level_one, level_two, _ = spots[c]
                 gone = (
                     gone_here
                     + jnp.where(level_one * V + lane > 0, serve_one, 0.0)
@@ -400,40 +427,53 @@
                 blocks = [field[c, s, q] for s in range(S)]
                 for s in range(S):
                     here = blocks[s]
-                    block = c * S + s
-                    value = here + back[block * U : (block + 1) * U]
-                    left = jnp.broadcast_to(beside_row(edge, places[2], low_at, s, q), (U, V))
-                    right = jnp.broadcast_to(beside_row(edge, places[3], up_at, s, q), (U, V))
-                    before = jnp.where(line == 0, left, pltpu.roll(here, 1, 0))
-                    after = jnp.where(line == U - 1, right, pltpu.roll(here, U - 1, 0))
+                    before = jnp.where(line == 0, 0.0, pltpu.roll(here, 1, 0))
+                    after = jnp.where(line == U - 1, 0.0, pltpu.roll(here, U - 1, 0))
                     moved = jnp.where(lane == V - 1, 0.0, pltpu.roll(before, V - 1, 1))
+                    value = here - (gone + (feed[s] + total_out[s])) * here
                     value = value + serve_one * moved + serve_two * after + feed[s] * before
-                    value = value - (gone + (feed[s] + total_out[s])) * here
                     for k in range(local_bits):
                         rate = turn_on[k] if s >> k & 1 else turn_off[k]
                         value = value + rate * blocks[s ^ (1 << k)]
-                    if step == 0:
-                        mixed[c, s, q] = value
-                    else:
+                    if step == 1:
                         if singles:
                             shifted = jnp.zeros((U, V), jnp.float32)
-                            first = jnp.zeros((1, V), jnp.float32)
                             for k in range(singles):
                                 other = far[k, c, s, q]
                                 shifted = shifted + shift_in[k] * other
-                                first = first + shift_in[k] * (
-                                    far_left[k, c, pl.ds(s * Q + q, 1), :]
-                                )
                                 value = value + stay_in[k] * other
-                            shifted = jnp.where(
-                                line == 0,
-                                jnp.broadcast_to(first, (U, V)),
-                                pltpu.roll(shifted, 1, 0),
-                            )
+                            shifted = jnp.where(line == 0, 0.0, pltpu.roll(shifted, 1, 0))
                             value = value + shifted + back_in * x_ref[c, s, q]
                         for k in range(singles, len(masks)):
                             value = value + pair_in[k - singles] * far[k, c, s, q]
-                        out_ref[c, s, q] = jnp.where(filled > 0, value, 0.0)
+                    result[c, s, q] = value
+            return carry
+
+        lax.fori_loop(0, Q, one, 0)
+
+    def add_rows(step, edge, result):
+        lane = lax.broadcasted_iota(jnp.int32, (Q, V), 1)
+        for c in range(C):
+            places = spots[c][0]
+            for s in range(S):
+                left = beside(edge, places[2], low_at, s)
+                right = beside(edge, places[3], up_at, s)
+                moved = jnp.where(lane == V - 1, 0.0, pltpu.roll(left, V - 1, 1))
+                added = feed[s] * left + serve_one * moved
+                if step == 1:
+                    for k in range(singles):
+                        added = added + shift_in[k] * far_left[k, c, s * Q : (s + 1) * Q, :]
+                result[c, s, :, 0, :] = result[c, s, :, 0, :] + added
+                result[c, s, :, U - 1, :] = result[c, s, :, U - 1, :] + serve_two * right
+
+    def finish(step, result):
+        def one(q, carry):
+            back = conv[q].T.reshape(C, S, U, V)
+            for c in range(C):
+                value = result[c, :, q] + back[c]
+                if step == 1:
+                    value = jnp.where(spots[c][3] > 0, value, 0.0)
+                result[c, :, q] = value
             return carry
 
         lax.fori_loop(0, Q, one, 0)
@@ -441,28 +481,27 @@
     for copy in x_near:
         copy.wait_recv()
     turn_near(0)
-    if n_level > 1:
-        end_hop(0, edge_one, 0)
+    end_hops(0, edge_one, 0, 1)
+    combine(0, x_ref, mixed)
+    end_hops(0, edge_one, 1, 2)
     lax.fori_loop(1, V // B, multiply, 0)
-    for h in range(1, n_level - 1):
-        end_hop(0, edge_one, h)
+    end_hops(0, edge_one, 2, n_level)
     pick_copies = take_rims(0, edge_one, rim_one)
     add_above(edge_one)
-
-    def keep_left(q, carry):
-        for c in range(C):
-            for s in range(S):
-                left_own[c, pl.ds(s * Q + q, 1), :] = beside_row(
-                    edge_one, spots[c][0][2], low_at, s, q
-                )
-        return carry
-
-    lax.fori_loop(0, Q, keep_left, 0)
-    left_copies = [
-        send(left_own, far_left.at[m], (far_left_send, far_left_recv), m, device)
-        for m, device in enumerate(fars[:singles])
-    ]
-    combine(0, edge_one, x_ref)
+    finish(0, mixed)
+    add_rows(0, edge_one, mixed)
+
+    def add_far_edges(part):
+        for k in range(singles):
+            edge_two[level, parts[part]] = (
+                edge_two[level, parts[part]] + twice[k] * far_edge[k, parts[part]]
+            )
+        start_hop(1, edge_two, part)
+
+    keep_rows(edge_two, mixed)
+    for copy in edge_copies:
+        copy.wait_recv()
+    add_far_edges(0)
 
     def turn_edges(i, carry):
         turned = [turn(mixed, i, g) for g in range(G)]
@@ -471,32 +510,36 @@
         return carry
 
     lax.fori_loop(0, groups, turn_edges, 0)
-    keep_rows(edge_two, rim_mixed, mixed)
-    for k, copy in enumerate(edge_copies):
-        copy.wait_recv()
-        edge_two[level] = edge_two[level] + twice[k] * far_edge[k]
-    start_hop(1, edge_two, 0)
+    keep_last(edge_two, rim_mixed)
+    add_far_edges(1)
+
+    for c in range(C):
+        for s in range(S):
+            left_own[c, s * Q : (s + 1) * Q, :] = beside(edge_one, spots[c][0][2], low_at, s)
+    left_copies = [
+        send(left_own, far_left.at[m], (far_left_send, far_left_recv), m, device)
+        for m, device in enumerate(fars[:singles])
+    ]
+
     mixed_near = []
     for s in range(S):
-        for m, copy in enumerate(far_copies[s]):
+        for copy in far_copies[s]:
             copy.wait_recv()
-        for c in range(C):
-
-            def add(q, carry):
+
+        def add(q, carry):
+            for c in range(C):
                 value = mixed[c, s, q]
                 for k in range(singles):
                     value = value + twice[k] * far[k, c, s, q]
                 mixed[c, s, q] = value
-                return carry
-
-            lax.fori_loop(0, Q, add, 0)
+            return carry
+
+        lax.fori_loop(0, Q, add, 0)
         for r, device in enumerate(cores):
             index = (n_phase - 1) * (1 + s) + r
             mixed_near.append(
                 send(mixed.at[:, s], near.at[1, r, :, s], near_sems, index, device)
             )
-        if s == 0 and n_level > 1:
-            end_hop(1, edge_two, 0)
 
     def turn_mixed(i, carry):
         turned = [turn(mixed, i, g) for g in range(G)]
@@ -505,20 +548,21 @@
         keep_rims(rim_two, i, turned)
         return carry
 
+    end_hops(1, edge_two, 0, 1)
     lax.fori_loop(0, groups, turn_mixed, 0)
-    if n_level > 2:
-        end_hop(1, edge_two, 1)
     for copy in mixed_near:
         copy.wait_recv()
     turn_near(1)
+    end_hops(1, edge_two, 1, 2)
+    combine(1, mixed, out_ref)
     lax.fori_loop(1, V // B, multiply, 0)
-    for h in range(2, n_level - 1):
-        end_hop(1, edge_two, h)
+    end_hops(1, edge_two, 2, n_level)
     pick_copies += take_rims(1, edge_two, rim_two)
     add_above(edge_two)
     for copy in left_copies:
         copy.wait_recv()
-    combine(1, edge_two, mixed)
+    add_rows(1, edge_two, out_ref)
+    finish(1, out_ref)
 
     for copy in x_near + mixed_near + pick_copies + left_copies + edge_copies:
         copy.wait_send()
@@ -554,9 +598,8 @@
     edge_rows = groups * batch + 2 * C * S * Q + C * (-(-groups // 8) * 8)
     f32, bf16 = jnp.float32, jnp.bfloat16
     vmem = pl.BlockSpec(memory_space=pltpu.VMEM)
-    smem = pl.BlockSpec(memory_space=pltpu.SMEM)
     singles, fars, cores = max(1, len(cross)), max(1, len(masks)), max(1, n_phase - 1)
-    counts = [fars * S, singles, singles, cores * (1 + S), 2 * cores, max(1, 4 * (n_level - 1))]
+    counts = [fars * S, singles, singles, cores * (1 + S), 2 * cores, max(1, 8 * (n_level - 1))]
     shapes = [
         ((fars,) + state_values.shape, f32),
         ((singles, edge_rows, lanes), f32),
@@ -578,17 +621,7 @@
         ((2, n_phase, C, groups, batch, lanes), f32),
         ((C, S * Q, V), f32),
     ]
-    return pl.pallas_call(
-        functools.partial(kernel, (n_level, n_phase, masks, local_bits, cross)),
-        out_shape=jax.ShapeDtypeStruct(state_values.shape, f32),
-        in_specs=[smem] * 5 + [vmem] * 3,
-        out_specs=vmem,
-        scratch_shapes=[pltpu.VMEM(*shape) for shape in shapes]
-        + [pltpu.SemaphoreType.DMA((n,)) for n in counts for _ in range(2)],
-        compiler_params=pltpu.CompilerParams(
-            collective_id=0, has_side_effects=True, vmem_limit_bytes=52 * 1024 * 1024
-        ),
-    )(
+    operands = (
         service_rates,
         source_rates,
         tile_levels,
@@ -598,6 +631,20 @@
         phase_rates,
         batch_rates,
     )
+    return pl.pallas_call(
+        functools.partial(kernel, (n_level, n_phase, masks, local_bits, cross)),
+        out_shape=jax.ShapeDtypeStruct(state_values.shape, f32),
+        in_specs=[pl.BlockSpec(memory_space=pl.ANY)] * 8,
+        out_specs=vmem,
+        scratch_shapes=[pltpu.SMEM(a.shape, a.dtype) for a in operands[:5]]
+        + [pltpu.VMEM(a.shape, a.dtype) for a in operands[5:]]
+        + [pltpu.SemaphoreType.DMA((len(operands),))]
+        + [pltpu.VMEM(*shape) for shape in shapes]
+        + [pltpu.SemaphoreType.DMA((n,)) for n in counts for _ in range(2)],
+        compiler_params=pltpu.CompilerParams(
+            collective_id=0, has_side_effects=True, vmem_limit_bytes=52 * 1024 * 1024
+        ),
+    )(*operands)
 
 
 def solution(mesh):

time: 72.3 us -> 74 us (1.024)
  Pallas kernels: 64.7 us -> 66.4 us
    pallas_call x1, Pallas kernels: 64.7 us -> 66.4 us  [body(): pl.pallas_call(functools.partial(kernel, (n_level, n_phase, masks, local_...]
where the time goes in v3:
time: 74 us; the launch traced here: 72.7 us
  Pallas kernels  66.4 us (90%)
  local copies, waits for them, and re-layouts  6.24 us (8%)
    pallas_call x1, Pallas kernels, body(): pl.pallas_call(functools.partial(kernel, (n_level, n_phase, masks, local_...  66.4 us
    unnamed x14, local copies, waits for them, and re-layouts  6.24 us

profile of v3, /device:TPU:0, one launch (start us, length us, event | category | flops | bytes accessed | tf_op | source)
XLA Modules:
  0.0 72.7 jit_solution(6597398653337152660)
XLA Ops:
  0.0 0.8 %copy.9.refs_2_ = s32[8,2]{1,0:T(8,128)S(1)} copy(s32[8,2]{0,1:T(2,128)} %param.13) | data formatting | bytes 128 | tf_op args[5]
  0.8 0.0 copy-start
  0.8 0.9 %copy-done = f32[16,32,32]{2,1,0:T(8,128)S(1)} copy-done((f32[16,32,32]{2,1,0:T(8,128)S(1)}, f32[16,32,32]{2,1,0:T(8,128)}, u32[]{:S(2)}) %copy-start) | copy-done | bytes 65560
  1.7 0.0 copy-start.1
  1.7 0.7 copy-done.1
  2.4 0.0 copy-start.2
  2.4 0.7 copy-done.2
  3.1 0.0 copy-start.3
  3.1 0.7 copy-done.3
  3.8 0.0 copy-start.4
  3.8 0.7 copy-done.4
  4.4 0.0 copy-start.5
  4.4 0.7 copy-done.5
  5.1 66.4 %shard_map.82 = f32[3,4,16,16,128]{4,3,2,1,0:T(8,128)S(1)} custom-call(f32[2]{0:T(128)S(1)} %copy-done.4, f32[3,3]{1,0:T(4,128)S(1)} %copy-done.3, s32[8,2]{1,0:T(8,128)S(1)} %copy.9.refs_2_, s32[8,5]{1,0:T(8,128)S(1)} %copy-done.2, s32[8]{0:T(128)S(1)} %copy-done.5, f32[3,4,16,16,128]{4,3,2,1,0:T(8,128)} %refs_5_.1, f32[32,32]{1,0:T(8,128)S(1)} %copy-done.1, ...), custom_call_target="tpu_custom_call" | custom-call | tf_op jit(solution)/shard_map/pallas_call | solution.py:634
  71.5 1.1 %copy.11 = f32[3,4,16,16,128]{4,3,2,1,0:T(8,128)} copy(f32[3,4,16,16,128]{4,3,2,1,0:T(8,128)S(1)} %shard_map.82) | data formatting | bytes 3145728
Async XLA Ops:
  0.8 0.9 %copy-start = (f32[16,32,32]{2,1,0:T(8,128)S(1)}, f32[16,32,32]{2,1,0:T(8,128)}, u32[]{:S(2)}) copy-start(f32[16,32,32]{2,1,0:T(8,128)} %refs_7_.1) | copy-start | bytes 196612
  1.7 0.7 copy-start.1
  2.4 0.7 copy-start.2
  3.1 0.7 copy-start.3
  3.8 0.7 copy-start.4
  4.4 0.7 copy-start.5

commit v4 on v3

--- a/solution.py
+++ b/solution.py
@@ -79,12 +79,15 @@
     n_level, n_phase, masks, local_bits, cross = sizes
     singles = len(cross)
     C, S, Q, U, V = x_ref.shape
-    SU = S * U
-    CSU = C * SU
+    halves = 2 if S > 1 else 1
+    H = S // halves
+    HU = H * U
+    used = C * HU
+    stride = high.shape[-1] // halves
     B = rim_one.shape[-2]
-    G = rim_one.shape[-1] // SU
+    G = rim_one.shape[-1] // (S * U)
     groups = Q // G
-    lanes = G * SU
+    lanes = G * S * U
     phases = n_phase * Q
     wide = 2 * B
     low_at = 0
@@ -172,8 +175,22 @@
     x_near = [
         send(x_hbm, near.at[0, r], near_sems, r, device) for r, device in enumerate(cores)
     ]
+
+    def send_far(s):
+        return [
+            send(x_hbm.at[:, s], far.at[m, :, s], (far_send, far_recv), m * S + s, device)
+            for m, device in enumerate(fars)
+        ]
+
+    far_copies = [send_far(0)]
     for copy in fetches:
         copy.wait()
+
+    for h in range(halves):
+        if used < stride:
+            gap = (phases, B + V, stride - used)
+            high[:, :, h * stride + used : (h + 1) * stride] = jnp.zeros(gap, jnp.bfloat16)
+            low[:, :, h * stride + used : (h + 1) * stride] = jnp.zeros(gap, jnp.bfloat16)
 
     tile_count = owner.shape[0]
     spots = []
@@ -190,29 +207,33 @@
             slot = owner[jnp.maximum(route, 0)]
             at = lax.div(slot, jnp.int32(C))
             places.append((route >= 0, at, slot - at * C))
-        spots.append((places, levels[tile, 0], levels[tile, 1], filled))
+        spots.append((places, levels[0, tile], levels[1, tile], filled))
         count = count + filled
     last = jnp.maximum(count - 1, 0)
 
-    def turn(field, i, g):
-        return field[:, :, i * G + g].reshape(CSU, V).T
-
-    def put(first, i, g, turned):
+    def turn(field, h, i, g):
+        return field[:, h * H : (h + 1) * H, i * G + g].reshape(used, V).T
+
+    def put(first, h, i, g, turned):
         top, rest = split(turned)
-        high[first + i * G + g, B:, :] = top
-        low[first + i * G + g, B:, :] = rest
+        high[first + i * G + g, B:, h * stride : h * stride + used] = top
+        low[first + i * G + g, B:, h * stride : h * stride + used] = rest
+
+    def group_lanes(turned, rows, c):
+        return jnp.concatenate([t[rows, c * HU : (c + 1) * HU] for t in turned], axis=1)
 
     def keep_rims(rim, i, turned):
         for c in range(C):
-            part = slice(c * SU, (c + 1) * SU)
-            rim[c, i] = jnp.concatenate([t[V - B :, part] for t in turned], axis=1)
+            rim[c, i] = group_lanes(turned, slice(V - B, V), c)
 
     def keep_bots(edge, i, turned):
         for c in range(C):
-            part = slice(c * SU, (c + 1) * SU)
-            edge[level, pl.ds(bot_at + c * bot_rows + i, 1), :] = jnp.concatenate(
-                [t[0:1, part] for t in turned], axis=1
+            edge[level, pl.ds(bot_at + c * bot_rows + i, 1), :] = group_lanes(
+                turned, slice(0, 1), c
             )
+
+    def turn_all(field, i):
+        return [turn(field, h, i, g) for h in range(halves) for g in range(G)]
 
     def keep_rows(edge, field):
         for c in range(C):
@@ -231,9 +252,10 @@
                 )
 
     def turn_own(i, carry):
-        turned = [turn(x_ref, i, g) for g in range(G)]
-        for g in range(G):
-            put(0, i, g, turned[g])
+        turned = turn_all(x_ref, i)
+        for h in range(halves):
+            for g in range(G):
+                put(0, h, i, g, turned[h * G + g])
         keep_rims(rim_one, i, turned)
         keep_bots(edge_one, i, turned)
         return carry
@@ -247,13 +269,7 @@
         send(edge_one.at[level], far_edge.at[m], (far_edge_send, far_edge_recv), m, device)
         for m, device in enumerate(fars[:singles])
     ]
-    far_copies = [
-        [
-            send(x_hbm.at[:, s], far.at[m, :, s], (far_send, far_recv), m * S + s, device)
-            for m, device in enumerate(fars)
-        ]
-        for s in range(S)
-    ]
+    far_copies += [send_far(s) for s in range(1, S)]
 
     across = lax.broadcasted_iota(jnp.int32, (phases, phases), 0) == lax.broadcasted_iota(
         jnp.int32, (phases, phases), 1
@@ -325,30 +341,35 @@
 
     def multiply(v, carry):
         window = pl.ds(pl.multiple_of(v * B, B), wide)
-        top = high[:, window, :].reshape(phases * wide, CSU)
-        rest = low[:, window, :].reshape(phases * wide, CSU)
+        top = high[:, window, :].reshape(phases * wide, halves * stride)
+        rest = low[:, window, :].reshape(phases * wide, halves * stride)
         both = jnp.dot(band_cat[...], top, preferred_element_type=jnp.float32)
         third = jnp.dot(band_cat[0:M, :], rest, preferred_element_type=jnp.float32)
         total = both[0:M] + (both[M:] + third)
-        conv[:, pl.ds(pl.multiple_of(v * B, B), B), :] = total.reshape(Q, B, CSU)
+        conv[:, pl.ds(pl.multiple_of(v * B, B), B), :] = total.reshape(Q, B, halves * stride)
         return carry
 
-    def turn_near(step):
+    def turn_near(step, which):
         for r in range(n_phase - 1):
 
             def one(i, carry):
-                for g in range(G):
-                    put((r + 1) * Q, i, g, turn(near.at[step, r], i, g))
+                for h in which:
+                    for g in range(G):
+                        put((r + 1) * Q, h, i, g, turn(near.at[step, r], h, i, g))
                 return carry
 
             lax.fori_loop(0, groups, one, 0)
 
+    def by_half(values, h, g):
+        at = (h * G + g) * HU
+        return jnp.concatenate([v[:, at : at + HU] for v in values], axis=1)
+
     def spread(i, first, values):
-        for g in range(G):
-            whole = jnp.concatenate([v[:, g * SU : (g + 1) * SU] for v in values], axis=1)
-            top, rest = split(whole)
-            high[first + i * G + g, 0:B, :] = top
-            low[first + i * G + g, 0:B, :] = rest
+        for h in range(halves):
+            for g in range(G):
+                top, rest = split(by_half(values, h, g))
+                high[first + i * G + g, 0:B, h * stride : h * stride + used] = top
+                low[first + i * G + g, 0:B, h * stride : h * stride + used] = rest
 
     def take_rims(step, edge, rim):
         def pick(i, carry):
@@ -366,7 +387,7 @@
             return carry
 
         lax.fori_loop(0, groups, pick, 0)
-        copies = [
+        return [
             send(
                 picks.at[step, 0],
                 picks.at[step, r + 1],
@@ -376,6 +397,8 @@
             )
             for r, device in enumerate(cores)
         ]
+
+    def share_rims(step, copies):
         for r, copy in enumerate(copies):
             copy.wait_recv()
 
@@ -384,8 +407,6 @@
                 return carry
 
             lax.fori_loop(0, groups, take, 0)
-        multiply(0, 0)
-        return copies
 
     def add_above(edge):
         def one(i, carry):
@@ -399,10 +420,12 @@
                     found = jnp.broadcast_to(jnp.where(there, found, 0.0), (8, lanes))
                     rolled.append(pltpu.roll(found, amount, 1))
                 values.append(jnp.where(lane % U == 0, rolled[1], rolled[0]))
-            for g in range(G):
-                whole = jnp.concatenate([v[:, g * SU : (g + 1) * SU] for v in values], axis=1)
-                q = i * G + g
-                conv[q, V - 1 : V, :] = conv[q, V - 1 : V, :] + serve_one * whole[0:1]
+            for h in range(halves):
+                part = slice(h * stride, h * stride + used)
+                for g in range(G):
+                    whole = by_half(values, h, g)
+                    q = i * G + g
+                    conv[q, V - 1 : V, part] = conv[q, V - 1 : V, part] + serve_one * whole[0:1]
             return carry
 
         lax.fori_loop(0, groups, one, 0)
@@ -410,43 +433,73 @@
     def beside(edge, place, first, s):
         there, at, slot = place
         return jnp.where(there, edge[at, pl.ds(first + (slot * S + s) * Q, Q), :], 0.0)
+
+    def gone_from(c, q, line, lane):
+        _, level_one, level_two, _ = spots[c]
+        return (
+            leave[pl.ds(phase * Q + q, 1), :]
+            + jnp.where(level_one * V + lane > 0, serve_one, 0.0)
+            + jnp.where(level_two * U + line > 0, serve_two, 0.0)
+        )
+
+    def within(s, here, gone, line, lane):
+        before = jnp.where(line == 0, 0.0, pltpu.roll(here, 1, 0))
+        after = jnp.where(line == U - 1, 0.0, pltpu.roll(here, U - 1, 0))
+        moved = jnp.where(lane == V - 1, 0.0, pltpu.roll(before, V - 1, 1))
+        value = here - (gone + (feed[s] + total_out[s])) * here
+        return value + serve_one * moved + serve_two * after + feed[s] * before
+
+    def flip_rate(s, k):
+        return turn_on[k] if s >> k & 1 else turn_off[k]
 
     def combine(step, field, result):
         def one(q, carry):
             line = lax.broadcasted_iota(jnp.int32, (U, V), 0)
             lane = lax.broadcasted_iota(jnp.int32, (U, V), 1)
-            gone_here = leave[pl.ds(phase * Q + q, 1), :]
-
             for c in range(C):
-                _, level_one, level_two, _ = spots[c]
-                gone = (
-                    gone_here
-                    + jnp.where(level_one * V + lane > 0, serve_one, 0.0)
-                    + jnp.where(level_two * U + line > 0, serve_two, 0.0)
-                )
+                gone = gone_from(c, q, line, lane)
                 blocks = [field[c, s, q] for s in range(S)]
                 for s in range(S):
-                    here = blocks[s]
-                    before = jnp.where(line == 0, 0.0, pltpu.roll(here, 1, 0))
-                    after = jnp.where(line == U - 1, 0.0, pltpu.roll(here, U - 1, 0))
-                    moved = jnp.where(lane == V - 1, 0.0, pltpu.roll(before, V - 1, 1))
-                    value = here - (gone + (feed[s] + total_out[s])) * here
-                    value = value + serve_one * moved + serve_two * after + feed[s] * before
+                    value = within(s, blocks[s], gone, line, lane)
                     for k in range(local_bits):
-                        rate = turn_on[k] if s >> k & 1 else turn_off[k]
-                        value = value + rate * blocks[s ^ (1 << k)]
-                    if step == 1:
-                        if singles:
-                            shifted = jnp.zeros((U, V), jnp.float32)
-                            for k in range(singles):
-                                other = far[k, c, s, q]
-                                shifted = shifted + shift_in[k] * other
-                                value = value + stay_in[k] * other
-                            shifted = jnp.where(line == 0, 0.0, pltpu.roll(shifted, 1, 0))
-                            value = value + shifted + back_in * x_ref[c, s, q]
-                        for k in range(singles, len(masks)):
-                            value = value + pair_in[k - singles] * far[k, c, s, q]
+                        value = value + flip_rate(s, k) * blocks[s ^ (1 << k)]
+                    if step == 1 and singles:
+                        value = value + back_in * x_ref[c, s, q]
                     result[c, s, q] = value
+            return carry
+
+        lax.fori_loop(0, Q, one, 0)
+
+    def add_far(s):
+        def one(q, carry):
+            for c in range(C):
+                value = mixed[c, s, q]
+                for k in range(singles):
+                    value = value + twice[k] * far[k, c, s, q]
+                mixed[c, s, q] = value
+            return carry
+
+        lax.fori_loop(0, Q, one, 0)
+
+    def combine_far(s):
+        def one(q, carry):
+            line = lax.broadcasted_iota(jnp.int32, (U, V), 0)
+            lane = lax.broadcasted_iota(jnp.int32, (U, V), 1)
+            for c in range(C):
+                here = shifted = stay = jnp.zeros((U, V), jnp.float32)
+                for k in range(singles):
+                    other = far[k, c, s, q]
+                    here = here + twice[k] * other
+                    shifted = shifted + shift_in[k] * other
+                    stay = stay + stay_in[k] * other
+                for k in range(singles, len(masks)):
+                    stay = stay + pair_in[k - singles] * far[k, c, s, q]
+                value = within(s, here, gone_from(c, q, line, lane), line, lane) + stay
+                value = value + jnp.where(line == 0, 0.0, pltpu.roll(shifted, 1, 0))
+                out_ref[c, s, q] = out_ref[c, s, q] + value
+                for k in range(local_bits):
+                    t = s ^ (1 << k)
+                    out_ref[c, t, q] = out_ref[c, t, q] + flip_rate(t, k) * here
             return carry
 
         lax.fori_loop(0, Q, one, 0)
@@ -468,19 +521,20 @@
 
     def finish(step, result):
         def one(q, carry):
-            back = conv[q].T.reshape(C, S, U, V)
-            for c in range(C):
-                value = result[c, :, q] + back[c]
-                if step == 1:
-                    value = jnp.where(spots[c][3] > 0, value, 0.0)
-                result[c, :, q] = value
+            for h in range(halves):
+                back = conv[q, :, h * stride : (h + 1) * stride].T[0:used].reshape(C, H, U, V)
+                for c in range(C):
+                    value = result[c, h * H : (h + 1) * H, q] + back[c]
+                    if step == 1:
+                        value = jnp.where(spots[c][3] > 0, value, 0.0)
+                    result[c, h * H : (h + 1) * H, q] = value
             return carry
 
         lax.fori_loop(0, Q, one, 0)
 
     for copy in x_near:
         copy.wait_recv()
-    turn_near(0)
+    turn_near(0, range(halves))
     end_hops(0, edge_one, 0, 1)
     combine(0, x_ref, mixed)
     end_hops(0, edge_one, 1, 2)
@@ -488,8 +542,10 @@
     end_hops(0, edge_one, 2, n_level)
     pick_copies = take_rims(0, edge_one, rim_one)
     add_above(edge_one)
+    add_rows(0, edge_one, mixed)
+    share_rims(0, pick_copies)
+    multiply(0, 0)
     finish(0, mixed)
-    add_rows(0, edge_one, mixed)
 
     def add_far_edges(part):
         for k in range(singles):
@@ -504,7 +560,7 @@
     add_far_edges(0)
 
     def turn_edges(i, carry):
-        turned = [turn(mixed, i, g) for g in range(G)]
+        turned = turn_all(mixed, i)
         keep_rims(rim_mixed, i, turned)
         keep_bots(edge_two, i, turned)
         return carry
@@ -521,43 +577,47 @@
         for m, device in enumerate(fars[:singles])
     ]
 
+    combine(1, mixed, out_ref)
+    end_hops(1, edge_two, 0, 1)
+
+    def turn_mixed(h):
+        def one(i, carry):
+            for g in range(G):
+                turned = turn(mixed, h, i, g)
+                put(0, h, i, g, turned)
+                for c in range(C):
+                    at = (h * G + g) * HU
+                    rim_two[c, i, :, at : at + HU] = turned[V - B :, c * HU : (c + 1) * HU]
+            return carry
+
+        lax.fori_loop(0, groups, one, 0)
+
     mixed_near = []
     for s in range(S):
         for copy in far_copies[s]:
             copy.wait_recv()
-
-        def add(q, carry):
-            for c in range(C):
-                value = mixed[c, s, q]
-                for k in range(singles):
-                    value = value + twice[k] * far[k, c, s, q]
-                mixed[c, s, q] = value
-            return carry
-
-        lax.fori_loop(0, Q, add, 0)
+        add_far(s)
+        if s == 0:
+            end_hops(1, edge_two, 1, 2)
+        fresh = []
         for r, device in enumerate(cores):
             index = (n_phase - 1) * (1 + s) + r
-            mixed_near.append(
-                send(mixed.at[:, s], near.at[1, r, :, s], near_sems, index, device)
-            )
-
-    def turn_mixed(i, carry):
-        turned = [turn(mixed, i, g) for g in range(G)]
-        for g in range(G):
-            put(0, i, g, turned[g])
-        keep_rims(rim_two, i, turned)
-        return carry
-
-    end_hops(1, edge_two, 0, 1)
-    lax.fori_loop(0, groups, turn_mixed, 0)
-    for copy in mixed_near:
-        copy.wait_recv()
-    turn_near(1)
-    end_hops(1, edge_two, 1, 2)
-    combine(1, mixed, out_ref)
-    lax.fori_loop(1, V // B, multiply, 0)
-    end_hops(1, edge_two, 2, n_level)
-    pick_copies += take_rims(1, edge_two, rim_two)
+            fresh.append(send(mixed.at[:, s], near.at[1, r, :, s], near_sems, index, device))
+        mixed_near += fresh
+        if s == S - 1:
+            turn_mixed(halves - 1)
+            end_hops(1, edge_two, 2, n_level)
+            last_picks = take_rims(1, edge_two, rim_two)
+            pick_copies += last_picks
+        combine_far(s)
+        for copy in fresh:
+            copy.wait_recv()
+        if (s + 1) % H == 0:
+            if s < S - 1:
+                turn_mixed(s // H)
+            turn_near(1, [s // H])
+    share_rims(1, last_picks)
+    lax.fori_loop(0, V // B, multiply, 0)
     add_above(edge_two)
     for copy in left_copies:
         copy.wait_recv()
@@ -595,6 +655,8 @@
     group = min(Q, max(1, 128 // (S * U)))
     lanes = group * S * U
     groups = Q // group
+    halves = 2 if S > 1 else 1
+    width = halves * (-(-(C * S * U // halves) // 128) * 128)
     edge_rows = groups * batch + 2 * C * S * Q + C * (-(-groups // 8) * 8)
     f32, bf16 = jnp.float32, jnp.bfloat16
     vmem = pl.BlockSpec(memory_space=pltpu.VMEM)
@@ -606,9 +668,9 @@
         ((singles, C, S * Q, V), f32),
         ((2, cores) + state_values.shape, f32),
         (state_values.shape, f32),
-        ((phases, batch + V, C * S * U), bf16),
-        ((phases, batch + V, C * S * U), bf16),
-        ((Q, V, C * S * U), f32),
+        ((phases, batch + V, width), bf16),
+        ((phases, batch + V, width), bf16),
+        ((Q, V, width), f32),
         ((phases * 2 * batch, 128), f32),
         ((Q, batch, phases * 2 * batch), f32),
         ((2 * Q * batch, phases * 2 * batch), bf16),
@@ -624,7 +686,7 @@
     operands = (
         service_rates,
         source_rates,
-        tile_levels,
+        tile_levels.T,
         routes,
         tile_owner,
         state_values,
@@ -642,7 +704,7 @@
         + [pltpu.VMEM(*shape) for shape in shapes]
         + [pltpu.SemaphoreType.DMA((n,)) for n in counts for _ in range(2)],
         compiler_params=pltpu.CompilerParams(
-            collective_id=0, has_side_effects=True, vmem_limit_bytes=52 * 1024 * 1024
+            collective_id=0, has_side_effects=True, vmem_limit_bytes=60 * 1024 * 1024
         ),
     )(*operands)
 

time: 74 us -> 67.5 us (0.912); the launches traced: 72.7 us -> 67.4 us
  local copies, waits for them, and re-layouts: 6.24 us -> 2.65 us
  Pallas kernels: 66.4 us -> 64.7 us
    unnamed x14 -> x1, local copies, waits for them, and re-layouts: 6.24 us -> 2.65 us
    pallas_call x1, Pallas kernels: 66.4 us -> 64.7 us  [body(): pl.pallas_call(functools.partial(kernel, (n_level, n_phase, masks, local_...]
where the time goes in v4:
time: 67.5 us; the launch traced here: 67.4 us
  Pallas kernels  64.7 us (96%)
  local copies, waits for them, and re-layouts  2.65 us (4%)
    pallas_call x1, Pallas kernels, body(): pl.pallas_call(functools.partial(kernel, (n_level, n_phase, masks, local_...  64.7 us
    unnamed x1, local copies, waits for them, and re-layouts  2.65 us

profile of v4, /device:TPU:0, one launch (start us, length us, event | category | flops | bytes accessed | tf_op | source)
XLA Modules:
  0.0 67.4 jit_solution(8717319228448960230)
XLA Ops:
  0.0 64.7 %shard_map.82 = f32[3,4,16,16,128]{4,3,2,1,0:T(8,128)} custom-call(f32[2]{0:T(128)} %refs_0_.1, f32[3,3]{1,0:T(4,128)} %refs_1_.1, s32[2,8]{1,0:T(2,128)} %bitcast.1, s32[8,5]{1,0:T(8,128)} %refs_3_.1, s32[8]{0:T(128)} %refs_4_.1, f32[3,4,16,16,128]{4,3,2,1,0:T(8,128)} %refs_5_.1, f32[32,32]{1,0:T(8,128)} %refs_6_.1, f32[16,32,32]{2,1,0:T(8,128)} %refs_7_.1), custom_call_target="tpu_custom_call" | custom-call | tf_op jit(solution)/shard_map/pallas_call | solution.py:696
  64.7 2.7 %copy.10 = f32[3,4,16,16,128]{4,3,2,1,0:T(8,128)} copy(f32[3,4,16,16,128]{4,3,2,1,0:T(8,128)} %shard_map.82) | data formatting | bytes 3145728

commit v5 on v4

--- a/solution.py
+++ b/solution.py
@@ -532,10 +532,10 @@
 
         lax.fori_loop(0, Q, one, 0)
 
+    end_hops(0, edge_one, 0, 1)
     for copy in x_near:
         copy.wait_recv()
     turn_near(0, range(halves))
-    end_hops(0, edge_one, 0, 1)
     combine(0, x_ref, mixed)
     end_hops(0, edge_one, 1, 2)
     lax.fori_loop(1, V // B, multiply, 0)
@@ -560,14 +560,22 @@
     add_far_edges(0)
 
     def turn_edges(i, carry):
-        turned = turn_all(mixed, i)
-        keep_rims(rim_mixed, i, turned)
-        keep_bots(edge_two, i, turned)
+        for c in range(C):
+            pieces = [
+                mixed[c, h * H : (h + 1) * H, i * G + g].reshape(HU, V)
+                for h in range(halves)
+                for g in range(G)
+            ]
+            turned = jnp.concatenate(pieces, axis=0).T
+            rim_mixed[c, i] = turned[V - B :]
+            edge_two[level, pl.ds(bot_at + c * bot_rows + i, 1), :] = turned[0:1]
         return carry
 
     lax.fori_loop(0, groups, turn_edges, 0)
     keep_last(edge_two, rim_mixed)
     add_far_edges(1)
+    if n_level > 1:
+        end_hop(1, edge_two, 0, 0)
 
     for c in range(C):
         for s in range(S):
@@ -578,7 +586,8 @@
     ]
 
     combine(1, mixed, out_ref)
-    end_hops(1, edge_two, 0, 1)
+    if n_level > 1:
+        end_hop(1, edge_two, 1, 0)
 
     def turn_mixed(h):
         def one(i, carry):
@@ -597,8 +606,6 @@
         for copy in far_copies[s]:
             copy.wait_recv()
         add_far(s)
-        if s == 0:
-            end_hops(1, edge_two, 1, 2)
         fresh = []
         for r, device in enumerate(cores):
             index = (n_phase - 1) * (1 + s) + r
@@ -606,9 +613,6 @@
         mixed_near += fresh
         if s == S - 1:
             turn_mixed(halves - 1)
-            end_hops(1, edge_two, 2, n_level)
-            last_picks = take_rims(1, edge_two, rim_two)
-            pick_copies += last_picks
         combine_far(s)
         for copy in fresh:
             copy.wait_recv()
@@ -616,12 +620,18 @@
             if s < S - 1:
                 turn_mixed(s // H)
             turn_near(1, [s // H])
-    share_rims(1, last_picks)
-    lax.fori_loop(0, V // B, multiply, 0)
+        if s == max(0, S // 2 - 1):
+            end_hops(1, edge_two, 1, 2)
+    lax.fori_loop(1, V // B, multiply, 0)
+    end_hops(1, edge_two, 2, n_level)
+    last_picks = take_rims(1, edge_two, rim_two)
+    pick_copies += last_picks
     add_above(edge_two)
     for copy in left_copies:
         copy.wait_recv()
     add_rows(1, edge_two, out_ref)
+    share_rims(1, last_picks)
+    multiply(0, 0)
     finish(1, out_ref)
 
     for copy in x_near + mixed_near + pick_copies + left_copies + edge_copies:

time: 67.5 us -> 63.4 us (0.939)
  Pallas kernels: 64.7 us -> 60.6 us
    pallas_call x1, Pallas kernels: 64.7 us -> 60.6 us  [body(): pl.pallas_call(functools.partial(kernel, (n_level, n_phase, masks, local_...]
where the time goes in v5:
time: 63.4 us; the launch traced here: 63.3 us
  Pallas kernels  60.6 us (96%)
  local copies, waits for them, and re-layouts  2.65 us (4%)
    pallas_call x1, Pallas kernels, body(): pl.pallas_call(functools.partial(kernel, (n_level, n_phase, masks, local_...  60.6 us
    unnamed x1, local copies, waits for them, and re-layouts  2.65 us

profile of v5, /device:TPU:0, one launch (start us, length us, event | category | flops | bytes accessed | tf_op | source)
XLA Modules:
  0.0 63.3 jit_solution(2279068759074621985)
XLA Ops:
  0.0 60.6 %shard_map.82 = f32[3,4,16,16,128]{4,3,2,1,0:T(8,128)} custom-call(f32[2]{0:T(128)} %refs_0_.1, f32[3,3]{1,0:T(4,128)} %refs_1_.1, s32[2,8]{1,0:T(2,128)} %bitcast.1, s32[8,5]{1,0:T(8,128)} %refs_3_.1, s32[8]{0:T(128)} %refs_4_.1, f32[3,4,16,16,128]{4,3,2,1,0:T(8,128)} %refs_5_.1, f32[32,32]{1,0:T(8,128)} %refs_6_.1, f32[16,32,32]{2,1,0:T(8,128)} %refs_7_.1), custom_call_target="tpu_custom_call" | custom-call | tf_op jit(solution)/shard_map/pallas_call | solution.py:706
  60.6 2.7 %copy.10 = f32[3,4,16,16,128]{4,3,2,1,0:T(8,128)} copy(f32[3,4,16,16,128]{4,3,2,1,0:T(8,128)} %shard_map.82) | data formatting | bytes 3145728

commit v6 on v5

--- a/solution.py
+++ b/solution.py
@@ -90,12 +90,15 @@
     lanes = G * S * U
     phases = n_phase * Q
     wide = 2 * B
-    low_at = 0
-    up_at = C * S * Q
     rim_at = 2 * C * S * Q
     bot_at = rim_at + groups * B
     bot_rows = (edge_one.shape[1] - bot_at) // C
-    parts = (pl.ds(0, rim_at), pl.ds(rim_at, edge_one.shape[1] - rim_at))
+    state_rows = 2 * C * Q
+    rim_part = pl.ds(rim_at, edge_one.shape[1] - rim_at)
+    parts = (
+        [pl.ds(0, rim_at), rim_part],
+        [pl.ds(s * state_rows, state_rows) for s in range(S)] + [rim_part],
+    )
     level, src, phase = (lax.axis_index(n) for n in ("level", "src", "phase"))
     cores = [{"phase": lax.rem(phase + r, n_phase)} for r in range(1, n_phase)]
     fars = [{"src": jnp.bitwise_xor(src, m)} for m in masks]
@@ -132,7 +135,7 @@
 
     def edge_copy(step, edge, part, way, h, block, toward):
         index = ((step * 2 + part) * 2 + way) * (n_level - 1) + h
-        piece = edge.at[block, parts[part]]
+        piece = edge.at[block, parts[step][part]]
         return make(piece, piece, (edge_send, edge_recv), index, {"level": level + toward})
 
     def hop(step, edge, part, way, h, act):
@@ -160,13 +163,13 @@
             if h < n_level - 2:
                 hop(step, edge, part, way, h + 1, lambda copy: copy.start())
 
-    def end_hops(step, edge, first, end):
+    def end_hops(step, edge, which, first, end):
         for h in range(first, min(end, n_level - 1)):
-            for part in range(2):
+            for part in which:
                 end_hop(step, edge, part, h)
 
     def end_sends(step, edge):
-        for part in range(2):
+        for part in range(len(parts[step])):
             for h in range(n_level - 1):
                 for way in range(2):
                     hop(step, edge, part, way, h, lambda copy: copy.wait_send())
@@ -235,12 +238,13 @@
     def turn_all(field, i):
         return [turn(field, h, i, g) for h in range(halves) for g in range(G)]
 
-    def keep_rows(edge, field):
-        for c in range(C):
-            for s in range(S):
-                at = (c * S + s) * Q
-                edge[level, low_at + at : low_at + at + Q, :] = field[c, s, :, U - 1, :]
-                edge[level, up_at + at : up_at + at + Q, :] = field[c, s, :, 0, :]
+    def keep_rows(edge, field, states):
+        for s in states:
+            for c in range(C):
+                at = s * state_rows + c * Q
+                edge[level, at : at + Q, :] = field[c, s, :, U - 1, :]
+                at = at + C * Q
+                edge[level, at : at + Q, :] = field[c, s, :, 0, :]
 
     def keep_last(edge, rim):
         edge[level, rim_at:bot_at, :] = rim[last].reshape(bot_at - rim_at, lanes)
@@ -260,13 +264,15 @@
         keep_bots(edge_one, i, turned)
         return carry
 
-    keep_rows(edge_one, x_ref)
+    keep_rows(edge_one, x_ref, range(S))
     start_hop(0, edge_one, 0)
     lax.fori_loop(0, groups, turn_own, 0)
     keep_last(edge_one, rim_one)
     start_hop(0, edge_one, 1)
     edge_copies = [
-        send(edge_one.at[level], far_edge.at[m], (far_edge_send, far_edge_recv), m, device)
+        send(
+            edge_one.at[level, rim_part], far_edge.at[m], (far_edge_send, far_edge_recv), m, device
+        )
         for m, device in enumerate(fars[:singles])
     ]
     far_copies += [send_far(s) for s in range(1, S)]
@@ -430,9 +436,10 @@
 
         lax.fori_loop(0, groups, one, 0)
 
-    def beside(edge, place, first, s):
+    def beside(edge, place, kind, s):
         there, at, slot = place
-        return jnp.where(there, edge[at, pl.ds(first + (slot * S + s) * Q, Q), :], 0.0)
+        first = s * state_rows + kind * C * Q
+        return jnp.where(there, edge[at, pl.ds(first + slot * Q, Q), :], 0.0)
 
     def gone_from(c, q, line, lane):
         _, level_one, level_two, _ = spots[c]
@@ -509,8 +516,8 @@
         for c in range(C):
             places = spots[c][0]
             for s in range(S):
-                left = beside(edge, places[2], low_at, s)
-                right = beside(edge, places[3], up_at, s)
+                left = beside(edge, places[2], 0, s)
+                right = beside(edge, places[3], 1, s)
                 moved = jnp.where(lane == V - 1, 0.0, pltpu.roll(left, V - 1, 1))
                 added = feed[s] * left + serve_one * moved
                 if step == 1:
@@ -532,32 +539,20 @@
 
         lax.fori_loop(0, Q, one, 0)
 
-    end_hops(0, edge_one, 0, 1)
+    end_hops(0, edge_one, range(2), 0, 1)
     for copy in x_near:
         copy.wait_recv()
     turn_near(0, range(halves))
     combine(0, x_ref, mixed)
-    end_hops(0, edge_one, 1, 2)
+    end_hops(0, edge_one, range(2), 1, 2)
     lax.fori_loop(1, V // B, multiply, 0)
-    end_hops(0, edge_one, 2, n_level)
+    end_hops(0, edge_one, range(2), 2, n_level)
     pick_copies = take_rims(0, edge_one, rim_one)
     add_above(edge_one)
     add_rows(0, edge_one, mixed)
     share_rims(0, pick_copies)
     multiply(0, 0)
     finish(0, mixed)
-
-    def add_far_edges(part):
-        for k in range(singles):
-            edge_two[level, parts[part]] = (
-                edge_two[level, parts[part]] + twice[k] * far_edge[k, parts[part]]
-            )
-        start_hop(1, edge_two, part)
-
-    keep_rows(edge_two, mixed)
-    for copy in edge_copies:
-        copy.wait_recv()
-    add_far_edges(0)
 
     def turn_edges(i, carry):
         for c in range(C):
@@ -573,21 +568,21 @@
 
     lax.fori_loop(0, groups, turn_edges, 0)
     keep_last(edge_two, rim_mixed)
-    add_far_edges(1)
-    if n_level > 1:
-        end_hop(1, edge_two, 0, 0)
+    for k, copy in enumerate(edge_copies):
+        copy.wait_recv()
+        edge_two[level, rim_part] = edge_two[level, rim_part] + twice[k] * far_edge[k]
+    start_hop(1, edge_two, S)
 
     for c in range(C):
         for s in range(S):
-            left_own[c, s * Q : (s + 1) * Q, :] = beside(edge_one, spots[c][0][2], low_at, s)
+            left_own[c, s * Q : (s + 1) * Q, :] = beside(edge_one, spots[c][0][2], 0, s)
     left_copies = [
         send(left_own, far_left.at[m], (far_left_send, far_left_recv), m, device)
         for m, device in enumerate(fars[:singles])
     ]
 
     combine(1, mixed, out_ref)
-    if n_level > 1:
-        end_hop(1, edge_two, 1, 0)
+    end_hops(1, edge_two, [S], 0, 1)
 
     def turn_mixed(h):
         def one(i, carry):
@@ -611,19 +606,22 @@
             index = (n_phase - 1) * (1 + s) + r
             fresh.append(send(mixed.at[:, s], near.at[1, r, :, s], near_sems, index, device))
         mixed_near += fresh
+        keep_rows(edge_two, mixed, [s])
+        start_hop(1, edge_two, s)
+        end_hops(1, edge_two, [s - 1 if s else S], 1, 2)
         if s == S - 1:
             turn_mixed(halves - 1)
         combine_far(s)
+        end_hops(1, edge_two, [s], 0, 1)
         for copy in fresh:
             copy.wait_recv()
         if (s + 1) % H == 0:
             if s < S - 1:
                 turn_mixed(s // H)
             turn_near(1, [s // H])
-        if s == max(0, S // 2 - 1):
-            end_hops(1, edge_two, 1, 2)
+    end_hops(1, edge_two, [S - 1], 1, 2)
     lax.fori_loop(1, V // B, multiply, 0)
-    end_hops(1, edge_two, 2, n_level)
+    end_hops(1, edge_two, range(S + 1), 2, n_level)
     last_picks = take_rims(1, edge_two, rim_two)
     pick_copies += last_picks
     add_above(edge_two)
@@ -671,10 +669,10 @@
     f32, bf16 = jnp.float32, jnp.bfloat16
     vmem = pl.BlockSpec(memory_space=pltpu.VMEM)
     singles, fars, cores = max(1, len(cross)), max(1, len(masks)), max(1, n_phase - 1)
-    counts = [fars * S, singles, singles, cores * (1 + S), 2 * cores, max(1, 8 * (n_level - 1))]
+    counts = [fars * S, singles, singles, cores * (1 + S), 2 * cores, max(1, (6 + 2 * S) * (n_level - 1))]
     shapes = [
         ((fars,) + state_values.shape, f32),
-        ((singles, edge_rows, lanes), f32),
+        ((singles, edge_rows - 2 * C * S * Q, lanes), f32),
         ((singles, C, S * Q, V), f32),
         ((2, cores) + state_values.shape, f32),
         (state_values.shape, f32),

time: 63.4 us -> 71.3 us (1.12)
  Pallas kernels: 60.6 us -> 68.5 us
    pallas_call x1, Pallas kernels: 60.6 us -> 68.5 us  [body(): pl.pallas_call(functools.partial(kernel, (n_level, n_phase, masks, local_...]
where the time goes in v6:
time: 71.3 us; the launch traced here: 71.1 us
  Pallas kernels  68.5 us (96%)
  local copies, waits for them, and re-layouts  2.65 us (4%)
    pallas_call x1, Pallas kernels, body(): pl.pallas_call(functools.partial(kernel, (n_level, n_phase, masks, local_...  68.5 us
    unnamed x1, local copies, waits for them, and re-layouts  2.65 us

profile of v6, /device:TPU:0, one launch (start us, length us, event | category | flops | bytes accessed | tf_op | source)
XLA Modules:
  0.0 71.1 jit_solution(5163444882265821239)
XLA Ops:
  0.0 68.5 %shard_map.82 = f32[3,4,16,16,128]{4,3,2,1,0:T(8,128)} custom-call(f32[2]{0:T(128)} %refs_0_.1, f32[3,3]{1,0:T(4,128)} %refs_1_.1, s32[2,8]{1,0:T(2,128)} %bitcast.1, s32[8,5]{1,0:T(8,128)} %refs_3_.1, s32[8]{0:T(128)} %refs_4_.1, f32[3,4,16,16,128]{4,3,2,1,0:T(8,128)} %refs_5_.1, f32[32,32]{1,0:T(8,128)} %refs_6_.1, f32[16,32,32]{2,1,0:T(8,128)} %refs_7_.1), custom_call_target="tpu_custom_call" | custom-call | tf_op jit(solution)/shard_map/pallas_call | solution.py:704
  68.5 2.7 %copy.10 = f32[3,4,16,16,128]{4,3,2,1,0:T(8,128)} copy(f32[3,4,16,16,128]{4,3,2,1,0:T(8,128)} %shard_map.82) | data formatting | bytes 3145728

commit v7 on v5

--- a/solution.py
+++ b/solution.py
@@ -358,7 +358,7 @@
                         put((r + 1) * Q, h, i, g, turn(near.at[step, r], h, i, g))
                 return carry
 
-            lax.fori_loop(0, groups, one, 0)
+            lax.fori_loop(0, groups, one, 0, unroll=2)
 
     def by_half(values, h, g):
         at = (h * G + g) * HU
@@ -479,7 +479,7 @@
                 mixed[c, s, q] = value
             return carry
 
-        lax.fori_loop(0, Q, one, 0)
+        lax.fori_loop(0, Q, one, 0, unroll=2)
 
     def combine_far(s):
         def one(q, carry):
@@ -530,7 +530,7 @@
                     result[c, h * H : (h + 1) * H, q] = value
             return carry
 
-        lax.fori_loop(0, Q, one, 0)
+        lax.fori_loop(0, Q, one, 0, unroll=2)
 
     end_hops(0, edge_one, 0, 1)
     for copy in x_near:
@@ -599,7 +599,7 @@
                     rim_two[c, i, :, at : at + HU] = turned[V - B :, c * HU : (c + 1) * HU]
             return carry
 
-        lax.fori_loop(0, groups, one, 0)
+        lax.fori_loop(0, groups, one, 0, unroll=2)
 
     mixed_near = []
     for s in range(S):

time: 63.4 us -> 62 us (0.978)
  Pallas kernels: 60.6 us -> 59.2 us
    pallas_call x1, Pallas kernels: 60.6 us -> 59.2 us  [body(): pl.pallas_call(functools.partial(kernel, (n_level, n_phase, masks, local_...]
where the time goes in v7:
time: 62 us; the launch traced here: 61.9 us
  Pallas kernels  59.2 us (95%)
  local copies, waits for them, and re-layouts  2.65 us (4%)
    pallas_call x1, Pallas kernels, body(): pl.pallas_call(functools.partial(kernel, (n_level, n_phase, masks, local_...  59.2 us
    unnamed x1, local copies, waits for them, and re-layouts  2.65 us

profile of v7, /device:TPU:0, one launch (start us, length us, event | category | flops | bytes accessed | tf_op | source)
XLA Modules:
  0.0 61.9 jit_solution(13887998996324620609)
XLA Ops:
  0.0 59.2 %shard_map.82 = f32[3,4,16,16,128]{4,3,2,1,0:T(8,128)} custom-call(f32[2]{0:T(128)} %refs_0_.1, f32[3,3]{1,0:T(4,128)} %refs_1_.1, s32[2,8]{1,0:T(2,128)} %bitcast.1, s32[8,5]{1,0:T(8,128)} %refs_3_.1, s32[8]{0:T(128)} %refs_4_.1, f32[3,4,16,16,128]{4,3,2,1,0:T(8,128)} %refs_5_.1, f32[32,32]{1,0:T(8,128)} %refs_6_.1, f32[16,32,32]{2,1,0:T(8,128)} %refs_7_.1), custom_call_target="tpu_custom_call" | custom-call | tf_op jit(solution)/shard_map/pallas_call | solution.py:706
  59.2 2.7 %copy.10 = f32[3,4,16,16,128]{4,3,2,1,0:T(8,128)} copy(f32[3,4,16,16,128]{4,3,2,1,0:T(8,128)} %shard_map.82) | data formatting | bytes 3145728
